TPU v7x, 512 devices: a whole 4x8x8 slice. The times are simulated.
512 devices in a mesh: patch: 64 (over z, y_hi, x), head: 8 (over y_lo, core).
Axes of the slice: x: 4, y: 8 (y_hi: 2, y_lo: 4; y = y_hi * 4 + y_lo), z: 8, core: 2. Of those that a mesh axis runs over, the one named last changes fastest.
Arguments:
- inputs: bfloat16 [2, 2048, 3072], P(None, 'patch', 'head'), may hold values from -111 to 111
- stale_kv: bfloat16 [2, 2048, 2048], P(None, 'patch', 'head'), may hold values from -16 to 16
- w_qkv: bfloat16 [3072, 3, 2048], P(None, None, 'head'), may hold values from -4 to 4
- w_out: bfloat16 [2048, 3072], P('head', 'patch'), may hold values from -0.375 to 0.375
- mod_table: float32 [4, 3, 3072], P(None, None, 'head'), may hold values from -2 to 2
- step_ids: int32 [2], replicated, may hold values from 0 to 3
- slab_order: int32 [64], P('patch'), may hold values from 0 to 63, each once
Outputs:
- branch: bfloat16 [2, 2048, 3072], P(None, 'patch', 'head')
Inputs may be any that keep to these rules, and one draw needn't show every extreme that they name: `slab_order`: every slab number once.
All inputs are finite; a program needn't handle non-finite values.
Results may differ from a plain program's by a relative error of at most 0.02.
Values may be sent and summed in bfloat16 or wider, within the bound.
A program may use at most 64 MiB of HBM per device.

v0:
```python
import math

import jax
import jax.numpy as jnp
from jax import lax
from jax.sharding import PartitionSpec as P

DH = 128
STEPS = 2


def angle_tables(positions, head_size):
    half_size = head_size // 2
    frequency = 10000.0 ** (-(2.0 * jnp.arange(half_size, dtype=jnp.float32)) / head_size)
    angle_grid = positions.astype(jnp.float32)[:, None] * frequency[None, :]
    return (jnp.cos(angle_grid)[:, None, :], jnp.sin(angle_grid)[:, None, :])


def rotate(values, cos_table, sin_table):
    half_size = values.shape[-1] // 2
    front_half = values[..., :half_size]
    back_half = values[..., half_size:]
    return jnp.concatenate(
        [
            front_half * cos_table - back_half * sin_table,
            front_half * sin_table + back_half * cos_table,
        ],
        axis=-1,
    )


def body(inputs, stale_kv, w_qkv, w_out, mod_table, step_ids, slab_order):
    tok_rows = inputs.shape[1]
    feat_cols = inputs.shape[2]
    model_width = w_qkv.shape[0]
    head_cols = w_qkv.shape[2]
    heads_dev = head_cols // DH
    table_rows = mod_table.shape[0]
    inv_root = 1.0 / math.sqrt(DH)
    own_start = lax.axis_index("patch") * tok_rows
    positions = slab_order[0] * tok_rows + jnp.arange(tok_rows, dtype=jnp.int32)
    cos_table, sin_table = angle_tables(positions, DH)
    w_flat = w_qkv.reshape(model_width, 3 * head_cols)
    w_full = lax.all_gather(w_out, "patch", axis=1, tiled=True)
    previous = stale_kv
    results = []
    for step in range(STEPS):
        chooser = jnp.arange(table_rows, dtype=jnp.int32) == step_ids[step]
        modulation = jnp.sum(jnp.where(chooser[:, None, None], mod_table, 0.0), axis=0)
        hidden = inputs[step].astype(jnp.float32)
        statistics = lax.psum((jnp.sum(hidden, axis=1), jnp.sum(hidden * hidden, axis=1)), "head")
        row_mean = statistics[0][:, None] / model_width
        row_square = statistics[1][:, None] / model_width
        inv_scale = lax.rsqrt(row_square - row_mean * row_mean + 1e-06)
        normed = ((hidden - row_mean) * inv_scale * (1.0 + modulation[1]) + modulation[0]).astype(
            jnp.bfloat16
        )
        projected = jnp.dot(
            lax.all_gather(normed, "head", axis=1, tiled=True),
            w_flat,
            preferred_element_type=jnp.float32,
        ).reshape(tok_rows, 3, heads_dev, DH)
        queries = rotate(projected[:, 0], cos_table, sin_table).astype(jnp.bfloat16)
        fresh_k = rotate(projected[:, 1], cos_table, sin_table).astype(jnp.bfloat16)
        fresh_v = projected[:, 2].astype(jnp.bfloat16)
        own_scores = (
            jnp.einsum("qhd,khd->hqk", queries, fresh_k, preferred_element_type=jnp.float32)
            * inv_root
        )
        own_max = jnp.max(own_scores, axis=2, keepdims=True)
        own_weights = jnp.exp(own_scores - own_max)
        own_totals = jnp.sum(own_weights, axis=2, keepdims=True)
        own_weighted = jnp.einsum(
            "hqk,khd->hqd",
            own_weights.astype(jnp.bfloat16),
            fresh_v,
            preferred_element_type=jnp.float32,
        )
        block_rows = lax.all_gather(previous, "patch", axis=1, tiled=True)
        totals = own_totals
        weighted = own_weighted
        piece_rows = block_rows.shape[1]
        key_rows = block_rows[0].reshape(piece_rows, heads_dev, DH)
        value_rows = block_rows[1].reshape(piece_rows, heads_dev, DH)
        scores = (
            jnp.einsum("qhd,khd->hqk", queries, key_rows, preferred_element_type=jnp.float32)
            * inv_root
        )
        row_ids = jnp.arange(piece_rows, dtype=jnp.int32)
        own_mask = (row_ids >= own_start) & (row_ids < own_start + tok_rows)
        scores = jnp.where(own_mask[None, None, :], -1e30, scores)
        new_max = jnp.maximum(own_max, jnp.max(scores, axis=2, keepdims=True))
        rescale = jnp.exp(own_max - new_max)
        weights = jnp.exp(scores - new_max)
        totals = totals * rescale + jnp.sum(weights, axis=2, keepdims=True)
        weighted = weighted * rescale + jnp.einsum(
            "hqk,khd->hqd",
            weights.astype(jnp.bfloat16),
            value_rows,
            preferred_element_type=jnp.float32,
        )
        attended = jnp.transpose((weighted / totals).astype(jnp.bfloat16), (1, 0, 2)).reshape(
            tok_rows, head_cols
        )
        partial_value = jnp.dot(attended, w_full, preferred_element_type=jnp.float32)
        summed = lax.psum(partial_value.astype(jnp.bfloat16), "head").astype(jnp.float32)
        own_cols = lax.dynamic_slice_in_dim(
            summed, lax.axis_index("head") * feat_cols, feat_cols, 1
        )
        results.append((modulation[2] * own_cols).astype(jnp.bfloat16))
        previous = jnp.stack(
            [fresh_k.reshape(tok_rows, head_cols), fresh_v.reshape(tok_rows, head_cols)]
        )
    return jnp.stack(results)


def solution(mesh):
    in_specs = (
        P(None, "patch", "head"),
        P(None, "patch", "head"),
        P(None, None, "head"),
        P("head", "patch"),
        P(None, None, "head"),
        P(),
        P("patch"),
    )
    out_specs = P(None, "patch", "head")
    return jax.shard_map(body, mesh=mesh, in_specs=in_specs, out_specs=out_specs, check_vma=False)
```

profile of v0, /device:TPU:1, one launch (start us, length us, event | category | flops | bytes accessed | tf_op | source)
XLA Modules:
  0.0 500.0 jit_solution(14808229929371773896)
XLA Ops:
  6.5 0.0 all-gather.4.cloned.1.call-start
  6.5 1.4 copy.26
  7.9 0.0 all-gather.4.cloned.1.call-update
  8.0 0.0 copy-start.2
  8.0 0.0 copy-start.4
  8.0 0.0 copy-start.3
  8.0 0.0 all-gather.8.cloned.1.call-start
  8.0 6.6 %copy.24 = bf16[3072,3,256]{0,2,1:T(8,128)(2,1)} copy(bf16[3072,3,256]{2,0,1:T(8,128)(2,1)} %param.9) | data formatting | bytes 9437184 | tf_op args[2]
  15.3 0.0 copy-done.2
  15.3 0.1 convert_reduce_fusion
  15.4 0.1 fusion.37
  15.6 19.9 %all-reduce = (f32[32]{0:T(128)S(1)}, f32[32]{0:T(128)S(1)}, f32[32]{0:T(128)S(1)}, f32[32]{0:T(128)S(1)}) all-reduce(f32[32]{0:T(128)S(1)} %get-tuple-element.8, f32[32]{0:T(128)S(1)} %get-tuple-element.6, f32[32]{0:T(128)S(1)} %get-tuple-element.7, f32[32]{0:T(128)S(1)} %get-tuple-element.5), channel_id=1, replica_groups=mesh['patch'=64,'head'=8] {'head'}, use_global_device_ids=true, to_apply=%region_4.5 | all-reduce | flops 128 | bytes 1024 | tf_op jit(solution)/shard_map/psum | solution.py:51
  35.4 0.0 copy-done.4
  35.4 0.6 fusion.71
  36.0 0.6 iota_compare_fusion.2
  36.7 0.7 iota_compare_fusion.3
  37.3 0.0 copy-done.3
  37.4 0.1 select_reduce_fusion
  37.5 0.1 fusion.36
  37.6 14.5 %all_gather.15 = bf16[32,3072]{1,0:T(8,128)(2,1)S(1)} all-gather(bf16[32,384]{1,0:T(8,128)(2,1)S(1)} %get-tuple-element.44), channel_id=1, replica_groups=mesh['patch'=64,'head'=8] {'head'}, dimensions={1}, use_global_device_ids=true | all-gather | bytes 221184 | tf_op jit(solution)/shard_map/all_gather | solution.py:59
  52.2 3.8 fusion.22
  56.1 0.1 multiply_cosine_fusion
  56.2 0.1 multiply_subtract_fusion
  56.3 0.1 maximum_convert_fusion
  56.5 0.6 pad_maximum_fusion.1
  57.1 0.0 all-gather.8.cloned.1.call-update
  57.1 0.0 all-gather.6.cloned.1.call-start
  57.2 0.7 all-gather.6.cloned.1.call-update
  57.9 0.0 all-reduce.4.cloned.1.call-start
  57.9 14.1 %all_gather.18 = bf16[32,3072]{1,0:T(8,128)(2,1)S(1)} all-gather(bf16[32,384]{1,0:T(8,128)(2,1)S(1)} %get-tuple-element.43), channel_id=1, replica_groups=mesh['patch'=64,'head'=8] {'head'}, dimensions={1}, use_global_device_ids=true | all-gather | bytes 221184 | tf_op jit(solution)/shard_map/all_gather | solution.py:59
  72.0 3.9 fusion.20
  76.0 0.1 subtract_convert_fusion.2
  76.1 0.2 fusion.74
  76.3 0.2 fusion.72
  76.6 70.3 %all-gather.4.cloned.1.call-done = bf16[2,2048,256]{2,0,1:T(2,128)(2,1)} async-done(((bf16[2,32,256]{2,0,1:T(2,128)(2,1)}), bf16[2,2048,256]{2,0,1:T(2,128)(2,1)}) %all-gather.4.cloned.1.call-update) | async-done | bytes 2097168 | tf_op jit(solution)/shard_map/all_gather | solution.py:79
  146.9 6.7 %fusion.69 = (bf16[1,2048,256]{2,0,1:T(2,128)(2,1)}, bf16[1,2048,256]{2,0,1:T(2,128)(2,1)S(1)}) fusion(bf16[2,2048,256]{2,0,1:T(2,128)(2,1)} %all-gather.4.cloned.1.call-done), kind=kLoop, calls=%fused_computation.127 | loop fusion | bytes 4194304 | tf_op jit(solution)/shard_map/slice | solution.py:83
  153.6 5.8 %copy.48 = bf16[1,2048,256]{1,2,0:T(8,128)(2,1)} copy(bf16[1,2048,256]{2,0,1:T(2,128)(2,1)} %get-tuple-element.27) | data formatting | bytes 2097152
  159.4 1.6 fusion.75
  161.0 4.2 copy.49
  165.3 115.8 %all-gather.8.cloned.1.call-done = bf16[2,2048,256]{2,1,0:T(8,128)(2,1)} async-done(((bf16[2,32,256]{2,1,0:T(8,128)(2,1)}), bf16[2,2048,256]{2,1,0:T(8,128)(2,1)}) %all-gather.8.cloned.1.call-update) | async-done | bytes 2097168 | tf_op jit(solution)/shard_map/all_gather | solution.py:79
  281.1 2.7 fusion.70
  283.8 1.4 copy.35
  285.3 0.0 copy-start
  285.3 1.7 fusion.73
  287.0 2.3 copy.37
  289.3 0.0 copy-start.1
  289.3 0.2 fusion.12
  289.5 0.0 copy-done
  289.5 0.5 convolution_bitcast_fusion.2
  290.0 0.2 fusion.11
  290.3 0.2 fusion.14
  290.5 0.0 copy-done.1
  290.5 0.5 convolution_bitcast_fusion
  291.0 0.2 fusion.10
  291.2 119.4 %all-gather.6.cloned.1.call-done = bf16[256,3072]{0,1:T(8,128)(2,1)} async-done(((bf16[256,48]{0,1:T(8,128)(2,1)}), bf16[256,3072]{0,1:T(8,128)(2,1)}) %all-gather.6.cloned.1.call-update) | async-done | bytes 1572880 | tf_op jit(solution)/shard_map/all_gather | solution.py:44
  410.6 2.7 convolution_convert_fusion.1
  413.3 2.7 convolution_convert_fusion
  415.9 0.0 all-reduce.4.cloned.1.call-update
  415.9 75.4 %all-reduce.4.cloned.1.call-done = (bf16[32,3072]{1,0:T(8,128)(2,1)}, bf16[32,3072]{1,0:T(8,128)(2,1)}) async-done(((bf16[32,3072]{1,0:T(8,128)(2,1)}, bf16[32,3072]{1,0:T(8,128)(2,1)}), (bf16[32,3072]{1,0:T(8,128)(2,1)}, bf16[32,3072]{1,0:T(8,128)(2,1)})) %all-reduce.4.cloned.1.call-update) | async-done | bytes 393232 | tf_op jit(solution)/shard_map/psum | solution.py:106
  491.4 0.7 fusion.42
  492.1 0.7 fusion.43
  492.8 0.6 pad_maximum_fusion
  (18 shorter events, 0.3 us)
Async XLA Ops:
  6.5 140.3 %all-gather.4.cloned.1.call-start = ((), (), s32[]{:S(2)}) async-start(), calls=%async_computation | async-start | bytes 2129920 | tf_op jit(solution)/shard_map/all_gather | solution.py:79
  8.0 7.4 %copy-start.2 = (bf16[2,32,384]{2,1,0:T(8,128)(2,1)S(1)}, bf16[2,32,384]{2,1,0:T(8,128)(2,1)}, u32[]{:S(2)}) copy-start(bf16[2,32,384]{2,1,0:T(8,128)(2,1)} %param.7) | copy-start | bytes 147460
  8.0 27.5 %copy-start.4 = (s32[2]{0:T(128)S(1)}, s32[2]{0:T(128)}, u32[]{:S(2)}) copy-start(s32[2]{0:T(128)} %param.12) | copy-start | bytes 28
  8.0 29.4 %copy-start.3 = (f32[4,3,384]{2,0,1:T(4,128)S(1)}, f32[4,3,384]{2,0,1:T(4,128)}, u32[]{:S(2)}) copy-start(f32[4,3,384]{2,0,1:T(4,128)} %param.11) | copy-start | bytes 55300
  8.0 273.1 %all-gather.8.cloned.1.call-start = ((), (), s32[]{:S(2)}) async-start(), calls=%async_computation.2 | async-start | bytes 2129920 | tf_op jit(solution)/shard_map/all_gather | solution.py:79
  57.1 353.5 %all-gather.6.cloned.1.call-start = ((), (), s32[]{:S(2)}) async-start(), calls=%async_computation.1 | async-start | bytes 1597440 | tf_op jit(solution)/shard_map/all_gather | solution.py:44
  57.9 433.5 %all-reduce.4.cloned.1.call-start = ((), (), s32[]{:S(2)}) async-start(), calls=%async_computation.3 | async-start | bytes 786432 | tf_op jit(solution)/shard_map/psum | solution.py:106
  285.3 4.3 copy-start
  289.3 1.2 copy-start.1
Sparse Core Ops, SparseCore 0:
  11.8 135.0 all-gather.3
  151.3 129.7 all-gather.7
  285.6 124.9 all-gather.5
  416.1 75.2 all-reduce.3
where the time goes:
time: 502 us; the launch traced here: 500 us
  waiting for transfers between devices  382 us (76%)
  blocking collectives  48.5 us (10%)
  local copies, waits for them, and re-layouts  32 us (6%)
  matrix products  18.2 us (4%)
  between operations  14 us (3%)
  other arithmetic  5.49 us (1%)
    all_gather x2, waiting for transfers between devices, body(): block_rows = lax.all_gather(previous, 'patch', axis=1, tiled=True)  186 us
    all_gather x1, waiting for transfers between devices, body(): w_full = lax.all_gather(w_out, 'patch', axis=1, tiled=True)  119 us
    psum x1, waiting for transfers between devices, body(): lax.psum(partial_value.astype(jnp.bfloat16), 'head').astype(jnp.float32)  75.4 us
    all_gather x2, blocking collectives, body(): lax.all_gather(normed, 'head', axis=1, tiled=True)  28.7 us
    psum x1, blocking collectives, body(): lax.psum((jnp.sum(hidden, axis=1), jnp.sum(hidden * hidden, axis=1)), 'he...  19.9 us
    unnamed x14, local copies, waits for them, and re-layouts  18.1 us
    slice x3, local copies, waits for them, and re-layouts, body(): key_rows = block_rows[0].reshape(piece_rows, heads_dev, DH)  10.9 us
  transfers between devices with their start and end apart: 4, of which 4 were waited for; matrix products, arithmetic and copies ran while one was open for 9% of the time, Pallas kernels for 0%

commit v1 on v0

v1 whole, which is shorter than its diff:
```python
import functools
import math

import jax
import jax.numpy as jnp
from jax import lax
from jax.experimental import pallas as pl
from jax.experimental.pallas import tpu as pltpu
from jax.sharding import PartitionSpec as P

DH = 128
TOK = 32
FEAT = 384
HC = 256
WIDTH = 3072
OUTC = 48
NZ, NYH, NX, NYL = 8, 2, 4, 4
NB = NYH * NX
F32 = jnp.float32
BF16 = jnp.bfloat16
MESH = pl.DeviceIdType.MESH


def dot_nt(a, b):
    return lax.dot_general(a, b, (((1,), (1,)), ((), ())), preferred_element_type=F32)


def dot_nn(a, b):
    return jnp.dot(a, b, preferred_element_type=F32)


def kernel(
    x_ref, stale_ref, w_ref, wo_ref, mod_ref, ids_ref, cos_ref, sin_ref, out_ref,
    w_v, xg, mg, a_v, kvs, kvf, kv1, qb, os_, orc, wo, e0s, e0r, e1s, e1r, acc,
    w_sem, xs_sem, xr_sem, ms_sem, mr_sem,
    ss_sem, sr_sem, fs_sem, fr_sem, qs_sem, qr_sem, os_sem, or_sem,
    wys_sem, wyr_sem, wzs_sem, wzr_sem, wxs_sem, wxr_sem,
    e0s_sem, e0r_sem, e1s_sem, e1r_sem,
):
    p = lax.axis_index("patch")
    h = lax.axis_index("head")
    z, b = p // NB, p % NB
    yh, x = b // NX, b % NX
    yl, c = h // 2, h % 2

    def z_peer(d):
        return (((z + d) % NZ) * NB + b, h)

    def x_peer(d):
        return (z * NB + yh * NX + (x + d) % NX, h)

    yh_peer = (z * NB + (1 - yh) * NX + x, h)
    sibling = (p, yl * 2 + 1 - c)

    def y_peer(d):
        return (p, ((yl + d) % NYL) * 2 + c)

    peers = [sibling, yh_peer]
    peers += [y_peer(d) for d in range(1, NYL)]
    peers += [x_peer(d) for d in range(1, NX)]
    peers += [z_peer(d) for d in range(1, NZ)]

    barrier = pltpu.get_barrier_semaphore()
    for peer in peers:
        pl.semaphore_signal(barrier, inc=1, device_id=peer, device_id_type=MESH)

    sent = []

    def send(src, dst, ssem, rsem, peer):
        copy = pltpu.make_async_remote_copy(
            src_ref=src, dst_ref=dst, send_sem=ssem, recv_sem=rsem, device_id=peer, device_id_type=MESH
        )
        copy.start()
        sent.append(copy)

    def arrived(dst, ssem, rsem, peer):
        pltpu.make_async_remote_copy(
            src_ref=dst, dst_ref=dst, send_sem=ssem, recv_sem=rsem, device_id=peer, device_id_type=MESH
        ).wait_recv()

    loads = [pltpu.make_async_copy(w_ref.at[t], w_v.at[t], w_sem.at[t]) for t in range(3)]
    for t in (1, 2, 0):
        loads[t].start()

    table_row = lax.broadcasted_iota(jnp.int32, (4, FEAT), 0)
    gates = []
    for s in range(2):
        pick = table_row == ids_ref[s]
        rows = [jnp.sum(jnp.where(pick, mod_ref[k], 0.0), axis=0, keepdims=True) for k in range(3)]
        mg[h, s : s + 1] = rows[0]
        mg[h, 2 + s : 3 + s] = rows[1]
        gates.append(rows[2])
    xg[h] = x_ref[...]
    kvs[0] = stale_ref[...]
    wo[z, yh, x] = wo_ref[...]

    pl.semaphore_wait(barrier, len(peers))

    for d in (2, 1, 3):
        send(xg.at[h], xg.at[h], xs_sem.at[d], xr_sem.at[h], y_peer(d))
        send(mg.at[h], mg.at[h], ms_sem.at[d], mr_sem.at[h], y_peer(d))
    send(xg.at[h], xg.at[h], xs_sem.at[0], xr_sem.at[h], sibling)
    send(mg.at[h], mg.at[h], ms_sem.at[0], mr_sem.at[h], sibling)
    send(wo.at[z, yh, x], wo.at[z, yh, x], wys_sem, wyr_sem, yh_peer)
    send(kvs.at[0], kvs.at[NX], ss_sem.at[0], sr_sem.at[NX], yh_peer)
    for d in range(1, NX):
        send(kvs.at[0], kvs.at[NX - d], ss_sem.at[d], sr_sem.at[NX - d], x_peer(d))

    for d in range(1, NYL):
        hs = ((yl + d) % NYL) * 2 + c
        arrived(xg.at[hs], xs_sem.at[d], xr_sem.at[hs], y_peer(d))
        arrived(mg.at[hs], ms_sem.at[d], mr_sem.at[hs], y_peer(d))
        send(xg.at[hs], xg.at[hs], xs_sem.at[NYL - 1 + d], xr_sem.at[hs], sibling)
        send(mg.at[hs], mg.at[hs], ms_sem.at[NYL - 1 + d], mr_sem.at[hs], sibling)

    arrived(wo.at[z, 1 - yh, x], wys_sem, wyr_sem, yh_peer)
    for d in (4, 3, 5, 2, 6, 1, 7):
        send(wo.at[z, :, x], wo.at[z, :, x], wzs_sem.at[d], wzr_sem.at[z], z_peer(d))
    arrived(kvs.at[NX], ss_sem.at[0], sr_sem.at[NX], yh_peer)
    for d in range(1, NX):
        send(kvs.at[NX], kvs.at[NX + NX - d], ss_sem.at[NX + d], sr_sem.at[NX + NX - d], x_peer(d))

    for d in range(NYL):
        hs = ((yl + d) % NYL) * 2 + 1 - c
        arrived(xg.at[hs], xs_sem.at[0], xr_sem.at[hs], sibling)
        arrived(mg.at[hs], ms_sem.at[0], mr_sem.at[hs], sibling)

    def forward_wo(d):
        zz = (z + d) % NZ
        if d:
            arrived(wo.at[zz, :, x], wzs_sem.at[d], wzr_sem.at[zz], z_peer(d))
        for e in range(1, NX):
            send(wo.at[zz, :, x], wo.at[zz, :, x], wxs_sem.at[d, e], wxr_sem.at[x, zz], x_peer(e))

    forward_wo(0)

    sum1 = jnp.zeros((2 * TOK, 128), F32)
    sum2 = jnp.zeros((2 * TOK, 128), F32)
    for j in range(8):
        v = xg[j].astype(F32)
        for k in range(FEAT // 128):
            part = v[:, k * 128 : (k + 1) * 128]
            sum1 += part
            sum2 += part * part
    mean = jnp.sum(sum1, axis=1, keepdims=True) / WIDTH
    square = jnp.sum(sum2, axis=1, keepdims=True) / WIDTH
    inv = lax.rsqrt(square - mean * mean + 1e-06)
    for j in range(8):
        v = (xg[j].astype(F32) - mean) * inv
        m = mg[j]
        for s in range(2):
            part = v[s * TOK : (s + 1) * TOK] * (1.0 + m[2 + s : 3 + s]) + m[s : s + 1]
            a_v[s * TOK : (s + 1) * TOK, j * FEAT : (j + 1) * FEAT] = part.astype(BF16)

    cos = jnp.concatenate([cos_ref[...]] * 2, axis=0)
    sin = jnp.concatenate([sin_ref[...]] * 2, axis=0)

    def rot(u):
        heads = []
        for i in range(2):
            uh = u[:, i * DH : (i + 1) * DH]
            heads.append(uh * cos + pltpu.roll(uh, DH // 2, 1) * sin)
        return jnp.concatenate(heads, axis=1).astype(BF16)

    loads[1].wait()
    kr = rot(dot_nn(a_v[...], w_v[1]))
    loads[2].wait()
    vr = dot_nn(a_v[...], w_v[2]).astype(BF16)
    kvf[0, 0] = kr[:TOK]
    kvf[0, 1] = vr[:TOK]
    kv1[0] = kr[TOK:]
    kv1[1] = vr[TOK:]
    send(kvf.at[0], kvf.at[NX], fs_sem.at[0], fr_sem.at[NX], yh_peer)
    for d in range(1, NX):
        send(kvf.at[0], kvf.at[NX - d], fs_sem.at[d], fr_sem.at[NX - d], x_peer(d))
    loads[0].wait()
    qb[0] = rot(dot_nn(a_v[...], w_v[0]))
    for d in (4, 3, 5, 2, 6, 1, 7):
        send(qb.at[0], qb.at[NZ - d], qs_sem.at[d], qr_sem.at[NZ - d], z_peer(d))

    arrived(kvf.at[NX], fs_sem.at[0], fr_sem.at[NX], yh_peer)
    for d in range(1, NX):
        send(kvf.at[NX], kvf.at[NX + NX - d], fs_sem.at[NX + d], fr_sem.at[NX + NX - d], x_peer(d))

    for d in (1, 7, 2, 6):
        forward_wo(d)

    inv_root = 1.0 / math.sqrt(DH)
    lane = lax.broadcasted_iota(jnp.int32, (NZ * TOK, 128), 1)
    ones = jnp.ones((NB * TOK, DH), BF16)

    def attend(s, held, own):
        outs, stats = [], jnp.zeros((NZ * TOK, 128), F32)
        for i in range(2):
            cols = slice(i * DH, (i + 1) * DH)
            keys = held[:, 0, :, cols].reshape(NB * TOK, DH)
            vals = held[:, 1, :, cols].reshape(NB * TOK, DH)
            own_keys = jnp.concatenate([own[0, :, cols], keys[TOK:]], axis=0)
            own_vals = jnp.concatenate([own[1, :, cols], vals[TOK:]], axis=0)
            q = qb[:, s * TOK : (s + 1) * TOK, cols].reshape(NZ * TOK, DH)
            scores = jnp.concatenate([dot_nt(q[:TOK], own_keys), dot_nt(q[TOK:], keys)], axis=0) * inv_root
            top = jnp.max(scores, axis=1, keepdims=True)
            weights = jnp.exp(scores - top).astype(BF16)
            mixed = jnp.concatenate(
                [
                    dot_nn(weights[:TOK], jnp.concatenate([own_vals, ones], axis=1)),
                    dot_nn(weights[TOK:], jnp.concatenate([vals, ones], axis=1)),
                ],
                axis=0,
            )
            total = mixed[:, DH:]
            outs.append((mixed[:, :DH] / total).astype(BF16))
            left = top + jnp.log(total)
            for k in range(3):
                piece = left.astype(BF16).astype(F32)
                stats = jnp.where(lane == 3 * i + k, piece, stats)
                left = left - piece
        full = jnp.concatenate(outs + [stats.astype(BF16)], axis=1).reshape(NZ, TOK, HC + 128)
        orc[s, 0] = full[0]
        for d in range(1, NZ):
            os_[s, d] = full[d]
        for d in (4, 3, 5, 2, 6, 1, 7):
            send(os_.at[s, d], orc.at[s, NZ - d], os_sem.at[s, d], or_sem.at[s, NZ - d], z_peer(d))

    for d in range(1, NX):
        arrived(kvs.at[d], ss_sem.at[d], sr_sem.at[d], x_peer(d))
        arrived(kvs.at[NX + d], ss_sem.at[NX + d], sr_sem.at[NX + d], x_peer(d))
    for d in range(1, NZ):
        arrived(qb.at[d], qs_sem.at[d], qr_sem.at[d], z_peer(d))
    attend(0, kvs, kvf.at[0])

    for d in (3, 5, 4):
        forward_wo(d)

    for d in range(1, NX):
        arrived(kvf.at[d], fs_sem.at[d], fr_sem.at[d], x_peer(d))
        arrived(kvf.at[NX + d], fs_sem.at[NX + d], fr_sem.at[NX + d], x_peer(d))
    attend(1, kvf, kv1)

    def merge(s):
        for d in range(1, NZ):
            arrived(orc.at[s, d], os_sem.at[s, d], or_sem.at[s, d], z_peer(d))
        heads = []
        for i in range(2):
            lse = []
            for d in range(NZ):
                st = orc[s, d, :, HC : HC + 128].astype(F32)
                k = 3 * i
                lse.append(st[:, k : k + 1] + st[:, k + 1 : k + 2] + st[:, k + 2 : k + 3])
            top = functools.reduce(jnp.maximum, lse)
            mixed = jnp.zeros((TOK, DH), F32)
            total = jnp.zeros((TOK, 1), F32)
            for d in range(NZ):
                weight = jnp.exp(lse[d] - top)
                total += weight
                mixed += weight * orc[s, d, :, i * DH : (i + 1) * DH].astype(F32)
            heads.append((mixed / total).astype(BF16))
        return jnp.concatenate(heads, axis=1)

    def block(o, j, core):
        return dot_nt(o, wo[((yl + j) % NYL) * 2 + core].reshape(FEAT, HC))

    def project(s):
        o = merge(s)
        if s == 0:
            for e in range(1, NX):
                for zz in range(NZ):
                    xs = (x + e) % NX
                    arrived(wo.at[zz, :, xs], wxs_sem.at[0, e], wxr_sem.at[xs, zz], x_peer(e))
        for j in (2, 1, 3, 0):
            e0s[s, j] = block(o, j, 1 - c).astype(BF16)
            send(e0s.at[s, j], e0r.at[s, j], e0s_sem.at[s, j], e0r_sem.at[s, j], sibling)
        for j in (2, 1, 3, 0):
            mine = block(o, j, c)
            arrived(e0r.at[s, j], e0s_sem.at[s, j], e0r_sem.at[s, j], sibling)
            mine = mine + e0r[s, j].astype(F32)
            if j:
                e1s[s, j] = mine.astype(BF16)
                send(e1s.at[s, j], e1r.at[s, NYL - j], e1s_sem.at[s, j], e1r_sem.at[s, NYL - j], y_peer(j))
            else:
                acc[s] = mine

    project(0)
    project(1)
    for s in range(2):
        total = acc[s]
        for j in range(1, NYL):
            arrived(e1r.at[s, j], e1s_sem.at[s, j], e1r_sem.at[s, j], y_peer(j))
            total = total + e1r[s, j].astype(F32)
        out_ref[s * TOK : (s + 1) * TOK] = (gates[s] * total).astype(BF16)

    for copy in sent:
        copy.wait_send()


def tables(slab_order):
    positions = slab_order[0] * TOK + jnp.arange(TOK, dtype=jnp.int32)
    half = DH // 2
    frequency = 10000.0 ** (-(2.0 * jnp.arange(half, dtype=F32)) / DH)
    angle = positions.astype(F32)[:, None] * frequency[None, :]
    cos, sin = jnp.cos(angle), jnp.sin(angle)
    return jnp.concatenate([cos, cos], axis=1), jnp.concatenate([-sin, sin], axis=1)


def body(inputs, stale_kv, w_qkv, w_out, mod_table, step_ids, slab_order):
    cos, sin = tables(slab_order)
    vmem = pl.BlockSpec(memory_space=pltpu.VMEM)
    dma = pltpu.SemaphoreType.DMA
    out = pl.pallas_call(
        kernel,
        out_shape=jax.ShapeDtypeStruct((2 * TOK, FEAT), BF16),
        in_specs=[
            vmem,
            vmem,
            pl.BlockSpec(memory_space=pl.ANY),
            vmem,
            vmem,
            pl.BlockSpec(memory_space=pltpu.SMEM),
            vmem,
            vmem,
        ],
        out_specs=vmem,
        scratch_shapes=[
            pltpu.VMEM((3, WIDTH, HC), BF16),
            pltpu.VMEM((8, 2 * TOK, FEAT), BF16),
            pltpu.VMEM((8, 4, FEAT), F32),
            pltpu.VMEM((2 * TOK, WIDTH), BF16),
            pltpu.VMEM((NB, 2, TOK, HC), BF16),
            pltpu.VMEM((NB, 2, TOK, HC), BF16),
            pltpu.VMEM((2, TOK, HC), BF16),
            pltpu.VMEM((NZ, 2 * TOK, HC), BF16),
            pltpu.VMEM((2, NZ, TOK, HC + 128), BF16),
            pltpu.VMEM((2, NZ, TOK, HC + 128), BF16),
            pltpu.VMEM((NZ, NYH, NX, OUTC, HC), BF16),
            pltpu.VMEM((2, NYL, TOK, FEAT), BF16),
            pltpu.VMEM((2, NYL, TOK, FEAT), BF16),
            pltpu.VMEM((2, NYL, TOK, FEAT), BF16),
            pltpu.VMEM((2, NYL, TOK, FEAT), BF16),
            pltpu.VMEM((2, TOK, FEAT), F32),
            dma((3,)),
            dma((7,)), dma((8,)), dma((7,)), dma((8,)),
            dma((8,)), dma((8,)), dma((8,)), dma((8,)),
            dma((8,)), dma((8,)), dma((2, 8)), dma((2, 8)),
            dma, dma, dma((8,)), dma((8,)), dma((8, 4)), dma((4, 8)),
            dma((2, 4)), dma((2, 4)), dma((2, 4)), dma((2, 4)),
        ],
        compiler_params=pltpu.CompilerParams(
            collective_id=0, has_side_effects=True, vmem_limit_bytes=40 * 1024 * 1024
        ),
        name="block",
    )(
        inputs.reshape(2 * TOK, FEAT),
        stale_kv,
        jnp.transpose(w_qkv, (1, 0, 2)),
        jnp.transpose(w_out),
        jnp.transpose(mod_table, (1, 0, 2)),
        step_ids,
        cos,
        sin,
    )
    return out.reshape(2, TOK, FEAT)


def solution(mesh):
    in_specs = (
        P(None, "patch", "head"),
        P(None, "patch", "head"),
        P(None, None, "head"),
        P("head", "patch"),
        P(None, None, "head"),
        P(),
        P("patch"),
    )
    out_specs = P(None, "patch", "head")
    return jax.shard_map(body, mesh=mesh, in_specs=in_specs, out_specs=out_specs, check_vma=False)
```

time: 502 us -> 67.8 us (0.14)
  waiting for transfers between devices: 382 us -> 0 us
  Pallas kernels: 0 us -> 59.9 us
  blocking collectives: 48.5 us -> 0 us
  local copies, waits for them, and re-layouts: 32 us -> 6.63 us
  matrix products: 18.2 us -> 0 us
  between operations: 14 us -> 0.68 us
  other arithmetic: 5.49 us -> 0.24 us
    all_gather x3 -> x0, waiting for transfers between devices: 305 us -> none  [the longest x2 186 us: body(): block_rows = lax.all_gather(previous, 'patch', axis=1, tiled=True)]
    psum x1 -> x0, waiting for transfers between devices: 75.4 us -> none  [body(): lax.psum(partial_value.astype(jnp.bfloat16), 'head').astype(jnp.float32)]
    pallas_call x0 -> x1, Pallas kernels: none -> 59.9 us  [body(): pl.pallas_call(kernel, out_shape=jax.ShapeDtypeStruct((2 * TOK, FEAT), BF...]
    all_gather x2 -> x0, blocking collectives: 28.7 us -> none  [body(): lax.all_gather(normed, 'head', axis=1, tiled=True)]
    psum x1 -> x0, blocking collectives: 19.9 us -> none  [body(): lax.psum((jnp.sum(hidden, axis=1), jnp.sum(hidden * hidden, axis=1)), 'he...]
    dot_general x12 -> x0, matrix products: 18.2 us -> none  [the longest x2 7.68 us: body(): jnp.dot(lax.all_gather(normed, 'head', axis=1, tiled=True), w_flat, prefe...]
    slice x6 -> x0, local copies, waits for them, and re-layouts: 13.8 us -> none  [the longest x3 10.9 us: body(): key_rows = block_rows[0].reshape(piece_rows, heads_dev, DH)]
    unnamed x14 -> x13, local copies, waits for them, and re-layouts: 18.1 us -> 6.63 us
  transfers between devices with their start and end apart: 4 -> 0, of which waited for: 4 -> 0; matrix products, arithmetic and copies ran while one was open for 9% -> 0% of each run, Pallas kernels for 0% -> 0%
where the time goes in v1:
time: 67.8 us; the launch traced here: 67.4 us
  Pallas kernels  59.9 us (88%)
  local copies, waits for them, and re-layouts  6.63 us (10%)
  between operations  0.68 us (1%)
    pallas_call x1, Pallas kernels, body(): pl.pallas_call(kernel, out_shape=jax.ShapeDtypeStruct((2 * TOK, FEAT), BF...  59.9 us
    unnamed x13, local copies, waits for them, and re-layouts  6.63 us

profile of v1, /device:TPU:1, one launch (start us, length us, event | category | flops | bytes accessed | tf_op | source)
XLA Modules:
  0.0 67.4 jit_solution(8659129161821075615)
XLA Ops:
  0.7 0.1 fusion
  0.8 0.1 pad_maximum_fusion
  0.9 0.0 copy-start
  0.9 2.3 %copy-done = bf16[3072,3,256]{2,0,1:T(8,128)(2,1)S(1)} copy-done((bf16[3072,3,256]{2,0,1:T(8,128)(2,1)S(1)}, bf16[3072,3,256]{2,0,1:T(8,128)(2,1)}, u32[]{:S(2)}) %copy-start) | copy-done | bytes 4718616
  3.3 0.0 copy-start.1
  3.3 0.8 %copy-done.1 = bf16[2,32,384]{2,1,0:T(8,128)(2,1)S(1)} copy-done((bf16[2,32,384]{2,1,0:T(8,128)(2,1)S(1)}, bf16[2,32,384]{2,1,0:T(8,128)(2,1)}, u32[]{:S(2)}) %copy-start.1) | copy-done | bytes 49176
  4.0 0.0 copy-start.2
  4.1 0.8 %copy-done.2 = bf16[2,32,256]{2,1,0:T(8,128)(2,1)S(1)} copy-done((bf16[2,32,256]{2,1,0:T(8,128)(2,1)S(1)}, bf16[2,32,256]{2,1,0:T(8,128)(2,1)}, u32[]{:S(2)}) %copy-start.2) | copy-done | bytes 32792
  4.8 0.0 copy-start.3
  4.8 0.7 %copy-done.3 = bf16[256,48]{0,1:T(8,128)(2,1)S(1)} copy-done((bf16[256,48]{0,1:T(8,128)(2,1)S(1)}, bf16[256,48]{0,1:T(8,128)(2,1)}, u32[]{:S(2)}) %copy-start.3) | copy-done | bytes 24600
  5.5 0.0 copy-start.4
  5.5 0.7 %copy-done.4 = f32[4,3,384]{2,0,1:T(4,128)S(1)} copy-done((f32[4,3,384]{2,0,1:T(4,128)S(1)}, f32[4,3,384]{2,0,1:T(4,128)}, u32[]{:S(2)}) %copy-start.4) | copy-done | bytes 18456
  6.3 0.0 copy-start.5
  6.3 0.7 copy-done.5
  6.9 59.9 %block.1 = bf16[64,384]{1,0:T(8,128)(2,1)S(1)} custom-call(bf16[64,384]{1,0:T(8,128)(2,1)S(1)} %bitcast.8, bf16[2,32,256]{2,1,0:T(8,128)(2,1)S(1)} %copy-done.2, bf16[3,3072,256]{2,1,0:T(8,128)(2,1)S(1)} %bitcast.6, bf16[48,256]{1,0:T(8,128)(2,1)S(1)} %bitcast.9, f32[3,4,384]{2,1,0:T(4,128)S(1)} %bitcast.10, s32[2]{0:T(128)S(1)} %copy-done.5, ...), custom_call_target="tpu_custom_call" | custom-call | tf_op jit(solution)/shard_map/block/pallas_call | solution.py:309
  66.8 0.6 copy.10
  (2 shorter events, 0.0 us)
Async XLA Ops:
  0.9 2.3 %copy-start = (bf16[3072,3,256]{2,0,1:T(8,128)(2,1)S(1)}, bf16[3072,3,256]{2,0,1:T(8,128)(2,1)}, u32[]{:S(2)}) copy-start(bf16[3072,3,256]{2,0,1:T(8,128)(2,1)} %param.9) | copy-start | bytes 14155780
  3.3 0.8 %copy-start.1 = (bf16[2,32,384]{2,1,0:T(8,128)(2,1)S(1)}, bf16[2,32,384]{2,1,0:T(8,128)(2,1)}, u32[]{:S(2)}) copy-start(bf16[2,32,384]{2,1,0:T(8,128)(2,1)} %param.7) | copy-start | bytes 147460
  4.0 0.8 %copy-start.2 = (bf16[2,32,256]{2,1,0:T(8,128)(2,1)S(1)}, bf16[2,32,256]{2,1,0:T(8,128)(2,1)}, u32[]{:S(2)}) copy-start(bf16[2,32,256]{2,1,0:T(8,128)(2,1)} %stale_ref.1) | copy-start | bytes 98308
  4.8 0.7 %copy-start.3 = (bf16[256,48]{0,1:T(8,128)(2,1)S(1)}, bf16[256,48]{0,1:T(8,128)(2,1)}, u32[]{:S(2)}) copy-start(bf16[256,48]{0,1:T(8,128)(2,1)} %param.10) | copy-start | bytes 73732
  5.5 0.7 %copy-start.4 = (f32[4,3,384]{2,0,1:T(4,128)S(1)}, f32[4,3,384]{2,0,1:T(4,128)}, u32[]{:S(2)}) copy-start(f32[4,3,384]{2,0,1:T(4,128)} %param.11) | copy-start | bytes 55300
  6.3 0.7 copy-start.5

commit v2 on v1

--- a/solution.py
+++ b/solution.py
@@ -31,8 +31,8 @@
 
 def kernel(
     x_ref, stale_ref, w_ref, wo_ref, mod_ref, ids_ref, cos_ref, sin_ref, out_ref,
-    w_v, xg, mg, a_v, kvs, kvf, kv1, qb, os_, orc, wo, e0s, e0r, e1s, e1r, acc,
-    w_sem, xs_sem, xr_sem, ms_sem, mr_sem,
+    ids_v, mod_v, w_v, xg, mg, a_v, kvs, kvf, kv1, qb, os_, orc, wo, e0s, e0r, e1s, e1r, acc,
+    in_sem, w_sem, xs_sem, xr_sem, ms_sem, mr_sem,
     ss_sem, sr_sem, fs_sem, fr_sem, qs_sem, qr_sem, os_sem, or_sem,
     wys_sem, wyr_sem, wzs_sem, wzr_sem, wxs_sem, wxr_sem,
     e0s_sem, e0r_sem, e1s_sem, e1r_sem,
@@ -78,21 +78,31 @@
             src_ref=dst, dst_ref=dst, send_sem=ssem, recv_sem=rsem, device_id=peer, device_id_type=MESH
         ).wait_recv()
 
+    small = [
+        pltpu.make_async_copy(ids_ref, ids_v, in_sem.at[0]),
+        pltpu.make_async_copy(mod_ref, mod_v, in_sem.at[1]),
+        pltpu.make_async_copy(x_ref, xg.at[h], in_sem.at[2]),
+        pltpu.make_async_copy(stale_ref, kvs.at[0], in_sem.at[3]),
+        pltpu.make_async_copy(wo_ref, wo.at[z, yh, x], in_sem.at[4]),
+    ]
+    for load in small:
+        load.start()
     loads = [pltpu.make_async_copy(w_ref.at[t], w_v.at[t], w_sem.at[t]) for t in range(3)]
     for t in (1, 2, 0):
         loads[t].start()
+    small[0].wait()
+    small[1].wait()
 
     table_row = lax.broadcasted_iota(jnp.int32, (4, FEAT), 0)
     gates = []
     for s in range(2):
-        pick = table_row == ids_ref[s]
-        rows = [jnp.sum(jnp.where(pick, mod_ref[k], 0.0), axis=0, keepdims=True) for k in range(3)]
+        pick = table_row == ids_v[s]
+        rows = [jnp.sum(jnp.where(pick, mod_v[k], 0.0), axis=0, keepdims=True) for k in range(3)]
         mg[h, s : s + 1] = rows[0]
         mg[h, 2 + s : 3 + s] = rows[1]
         gates.append(rows[2])
-    xg[h] = x_ref[...]
-    kvs[0] = stale_ref[...]
-    wo[z, yh, x] = wo_ref[...]
+    for load in small[2:]:
+        load.wait()
 
     pl.semaphore_wait(barrier, len(peers))
 
@@ -309,18 +319,11 @@
     out = pl.pallas_call(
         kernel,
         out_shape=jax.ShapeDtypeStruct((2 * TOK, FEAT), BF16),
-        in_specs=[
-            vmem,
-            vmem,
-            pl.BlockSpec(memory_space=pl.ANY),
-            vmem,
-            vmem,
-            pl.BlockSpec(memory_space=pltpu.SMEM),
-            vmem,
-            vmem,
-        ],
+        in_specs=[pl.BlockSpec(memory_space=pltpu.HBM)] * 6 + [vmem] * 2,
         out_specs=vmem,
         scratch_shapes=[
+            pltpu.SMEM((2,), jnp.int32),
+            pltpu.VMEM((3, 4, FEAT), F32),
             pltpu.VMEM((3, WIDTH, HC), BF16),
             pltpu.VMEM((8, 2 * TOK, FEAT), BF16),
             pltpu.VMEM((8, 4, FEAT), F32),
@@ -337,7 +340,7 @@
             pltpu.VMEM((2, NYL, TOK, FEAT), BF16),
             pltpu.VMEM((2, NYL, TOK, FEAT), BF16),
             pltpu.VMEM((2, TOK, FEAT), F32),
-            dma((3,)),
+            dma((5,)), dma((3,)),
             dma((7,)), dma((8,)), dma((7,)), dma((8,)),
             dma((8,)), dma((8,)), dma((8,)), dma((8,)),
             dma((8,)), dma((8,)), dma((2, 8)), dma((2, 8)),
@@ -345,7 +348,7 @@
             dma((2, 4)), dma((2, 4)), dma((2, 4)), dma((2, 4)),
         ],
         compiler_params=pltpu.CompilerParams(
-            collective_id=0, has_side_effects=True, vmem_limit_bytes=40 * 1024 * 1024
+            collective_id=0, has_side_effects=True, vmem_limit_bytes=60 * 1024 * 1024
         ),
         name="block",
     )(

time: 67.8 us -> 63.7 us (0.940)
  local copies, waits for them, and re-layouts: 6.63 us -> 1.42 us
    unnamed x13 -> x1, local copies, waits for them, and re-layouts: 6.63 us -> 1.42 us
where the time goes in v2:
time: 63.7 us; the launch traced here: 63.4 us
  Pallas kernels  60.4 us (95%)
  local copies, waits for them, and re-layouts  1.42 us (2%)
  other arithmetic  0.85 us (1%)
  between operations  0.68 us (1%)
    pallas_call x1, Pallas kernels, body(): pl.pallas_call(kernel, out_shape=jax.ShapeDtypeStruct((2 * TOK, FEAT), BF...  60.4 us
    unnamed x1, local copies, waits for them, and re-layouts  1.42 us

profile of v2, /device:TPU:1, one launch (start us, length us, event | category | flops | bytes accessed | tf_op | source)
XLA Modules:
  0.0 63.4 jit_solution(7359471309431955120)
XLA Ops:
  0.7 0.1 fusion
  0.8 0.7 %pad_maximum_fusion = (f32[32,128]{1,0:T(8,128)}, f32[32,128]{1,0:T(8,128)}) fusion(f32[32,64]{1,0:T(8,128)S(1)} %get-tuple-element.7, f32[32,64]{1,0:T(8,128)S(1)} %get-tuple-element.6, f32[32,64]{1,0:T(8,128)S(1)} %get-tuple-element.5), kind=kLoop, calls=%fused_computation.2 | loop fusion | flops 8192 | bytes 57344 | tf_op jit(solution)/shard_map/concatenate | solution.py:312
  1.5 60.4 %block.1 = bf16[64,384]{1,0:T(8,128)(2,1)} custom-call(bf16[64,384]{1,0:T(8,128)(2,1)} %bitcast.8, bf16[2,32,256]{2,1,0:T(8,128)(2,1)} %stale_ref.1, bf16[3,3072,256]{2,1,0:T(8,128)(2,1)} %bitcast.6, bf16[48,256]{1,0:T(8,128)(2,1)} %bitcast.9, f32[3,4,384]{2,1,0:T(4,128)} %bitcast.10, s32[2]{0:T(128)} %ids_ref.1, f32[32,128]{1,0:T(8,128)} %get-tuple-element.8.cos_ref, ...), custom_call_target="tpu_custom_call" | custom-call | tf_op jit(solution)/shard_map/block/pallas_call | solution.py:319
  62.0 1.4 %copy.10 = bf16[2,32,384]{2,1,0:T(8,128)(2,1)} copy(bf16[2,32,384]{2,1,0:T(8,128)(2,1)} %bitcast.7) | data formatting | bytes 98304
  (2 shorter events, 0.0 us)

commit v3 on v2

--- a/solution.py
+++ b/solution.py
@@ -16,6 +16,8 @@
 OUTC = 48
 NZ, NYH, NX, NYL = 8, 2, 4, 4
 NB = NYH * NX
+NK = NYH * NZ
+NEAR = (1, NZ - 1, 2, NZ - 2)
 F32 = jnp.float32
 BF16 = jnp.bfloat16
 MESH = pl.DeviceIdType.MESH
@@ -44,7 +46,7 @@
     yl, c = h // 2, h % 2
 
     def z_peer(d):
-        return (((z + d) % NZ) * NB + b, h)
+        return (((z + d % NZ) % NZ) * NB + b, h)
 
     def x_peer(d):
         return (z * NB + yh * NX + (x + d) % NX, h)
@@ -58,7 +60,7 @@
     peers = [sibling, yh_peer]
     peers += [y_peer(d) for d in range(1, NYL)]
     peers += [x_peer(d) for d in range(1, NX)]
-    peers += [z_peer(d) for d in range(1, NZ)]
+    peers += [z_peer(d) for d in NEAR]
 
     barrier = pltpu.get_barrier_semaphore()
     for peer in peers:
@@ -111,10 +113,62 @@
         send(mg.at[h], mg.at[h], ms_sem.at[d], mr_sem.at[h], y_peer(d))
     send(xg.at[h], xg.at[h], xs_sem.at[0], xr_sem.at[h], sibling)
     send(mg.at[h], mg.at[h], ms_sem.at[0], mr_sem.at[h], sibling)
+
+    def kv_near(buf, ssem, rsem, yrel):
+        base = yrel * NZ
+        for d in NEAR:
+            send(buf.at[base], buf.at[base + NZ - d], ssem.at[base + d], rsem.at[base + NZ - d], z_peer(d))
+
+    def kv_partner(buf, ssem, rsem):
+        send(buf.at[0], buf.at[NZ], ssem.at[0], rsem.at[NZ], yh_peer)
+
+    def kv_from_partner(buf, ssem, rsem):
+        arrived(buf.at[NZ], ssem.at[0], rsem.at[NZ], yh_peer)
+        kv_near(buf, ssem, rsem, 1)
+
+    def kv_far(buf, ssem, rsem, yrel):
+        base = yrel * NZ
+        arrived(buf.at[base + 2], ssem.at[base + 2], rsem.at[base + 2], z_peer(2))
+        send(buf.at[base + 2], buf.at[base + 3], ssem.at[base + 3], rsem.at[base + 3], z_peer(-1))
+        send(buf.at[base + 2, 0], buf.at[base + 4, 0], ssem.at[base + 4], rsem.at[base + 4], z_peer(-2))
+        arrived(buf.at[base + 6], ssem.at[base + 6], rsem.at[base + 6], z_peer(-2))
+        send(buf.at[base + 6], buf.at[base + 5], ssem.at[base + 5], rsem.at[base + 5], z_peer(1))
+        send(buf.at[base + 6, 1], buf.at[base + 4, 1], ssem.at[NK + yrel], rsem.at[NK + yrel], z_peer(2))
+
+    def kv_all(buf, ssem, rsem):
+        for yrel in range(NYH):
+            base = yrel * NZ
+            for d in (1, 7):
+                arrived(buf.at[base + d], ssem.at[base + d], rsem.at[base + d], z_peer(d))
+            arrived(buf.at[base + 3], ssem.at[base + 3], rsem.at[base + 3], z_peer(1))
+            arrived(buf.at[base + 5], ssem.at[base + 5], rsem.at[base + 5], z_peer(-1))
+            arrived(buf.at[base + 4, 0], ssem.at[base + 4], rsem.at[base + 4], z_peer(2))
+            arrived(buf.at[base + 4, 1], ssem.at[NK + yrel], rsem.at[NK + yrel], z_peer(-2))
+
+    def wo_near():
+        arrived(wo.at[z, 1 - yh, x], wys_sem, wyr_sem, yh_peer)
+        for d in NEAR:
+            send(wo.at[z, :, x], wo.at[z, :, x], wzs_sem.at[d], wzr_sem.at[z], z_peer(d))
+
+    def wo_take(d):
+        zz = (z + d) % NZ
+        if d == 4:
+            arrived(wo.at[zz, 0, x], wzs_sem.at[4], wzr_sem.at[zz], z_peer(2))
+            arrived(wo.at[zz, 1, x], wzs_sem.at[0], wzr_sem.at[NZ], z_peer(-2))
+        elif d:
+            arrived(wo.at[zz, :, x], wzs_sem.at[d], wzr_sem.at[zz], z_peer(d))
+        if d == 2:
+            send(wo.at[zz, :, x], wo.at[zz, :, x], wzs_sem.at[3], wzr_sem.at[zz], z_peer(-1))
+            send(wo.at[zz, 0, x], wo.at[zz, 0, x], wzs_sem.at[4], wzr_sem.at[zz], z_peer(-2))
+        if d == 6:
+            send(wo.at[zz, :, x], wo.at[zz, :, x], wzs_sem.at[5], wzr_sem.at[zz], z_peer(1))
+            send(wo.at[zz, 1, x], wo.at[zz, 1, x], wzs_sem.at[0], wzr_sem.at[NZ], z_peer(2))
+        for e in range(1, NX):
+            send(wo.at[zz, :, x], wo.at[zz, :, x], wxs_sem.at[d, e], wxr_sem.at[x, zz], x_peer(e))
+
+    kv_near(kvs, ss_sem, sr_sem, 0)
+    kv_partner(kvs, ss_sem, sr_sem)
     send(wo.at[z, yh, x], wo.at[z, yh, x], wys_sem, wyr_sem, yh_peer)
-    send(kvs.at[0], kvs.at[NX], ss_sem.at[0], sr_sem.at[NX], yh_peer)
-    for d in range(1, NX):
-        send(kvs.at[0], kvs.at[NX - d], ss_sem.at[d], sr_sem.at[NX - d], x_peer(d))
 
     for d in range(1, NYL):
         hs = ((yl + d) % NYL) * 2 + c
@@ -123,26 +177,15 @@
         send(xg.at[hs], xg.at[hs], xs_sem.at[NYL - 1 + d], xr_sem.at[hs], sibling)
         send(mg.at[hs], mg.at[hs], ms_sem.at[NYL - 1 + d], mr_sem.at[hs], sibling)
 
-    arrived(wo.at[z, 1 - yh, x], wys_sem, wyr_sem, yh_peer)
-    for d in (4, 3, 5, 2, 6, 1, 7):
-        send(wo.at[z, :, x], wo.at[z, :, x], wzs_sem.at[d], wzr_sem.at[z], z_peer(d))
-    arrived(kvs.at[NX], ss_sem.at[0], sr_sem.at[NX], yh_peer)
-    for d in range(1, NX):
-        send(kvs.at[NX], kvs.at[NX + NX - d], ss_sem.at[NX + d], sr_sem.at[NX + NX - d], x_peer(d))
+    kv_from_partner(kvs, ss_sem, sr_sem)
+    kv_far(kvs, ss_sem, sr_sem, 0)
+    wo_near()
+    wo_take(0)
 
     for d in range(NYL):
         hs = ((yl + d) % NYL) * 2 + 1 - c
         arrived(xg.at[hs], xs_sem.at[0], xr_sem.at[hs], sibling)
         arrived(mg.at[hs], ms_sem.at[0], mr_sem.at[hs], sibling)
-
-    def forward_wo(d):
-        zz = (z + d) % NZ
-        if d:
-            arrived(wo.at[zz, :, x], wzs_sem.at[d], wzr_sem.at[zz], z_peer(d))
-        for e in range(1, NX):
-            send(wo.at[zz, :, x], wo.at[zz, :, x], wxs_sem.at[d, e], wxr_sem.at[x, zz], x_peer(e))
-
-    forward_wo(0)
 
     sum1 = jnp.zeros((2 * TOK, 128), F32)
     sum2 = jnp.zeros((2 * TOK, 128), F32)
@@ -180,34 +223,34 @@
     kvf[0, 1] = vr[:TOK]
     kv1[0] = kr[TOK:]
     kv1[1] = vr[TOK:]
-    send(kvf.at[0], kvf.at[NX], fs_sem.at[0], fr_sem.at[NX], yh_peer)
-    for d in range(1, NX):
-        send(kvf.at[0], kvf.at[NX - d], fs_sem.at[d], fr_sem.at[NX - d], x_peer(d))
+    kv_near(kvf, fs_sem, fr_sem, 0)
+    kv_partner(kvf, fs_sem, fr_sem)
     loads[0].wait()
     qb[0] = rot(dot_nn(a_v[...], w_v[0]))
-    for d in (4, 3, 5, 2, 6, 1, 7):
-        send(qb.at[0], qb.at[NZ - d], qs_sem.at[d], qr_sem.at[NZ - d], z_peer(d))
-
-    arrived(kvf.at[NX], fs_sem.at[0], fr_sem.at[NX], yh_peer)
-    for d in range(1, NX):
-        send(kvf.at[NX], kvf.at[NX + NX - d], fs_sem.at[NX + d], fr_sem.at[NX + NX - d], x_peer(d))
-
-    for d in (1, 7, 2, 6):
-        forward_wo(d)
+    for d in (2, 1, 3):
+        send(qb.at[0], qb.at[NX - d], qs_sem.at[d], qr_sem.at[NX - d], x_peer(d))
+
+    kv_far(kvs, ss_sem, sr_sem, 1)
+    wo_take(2)
+    wo_take(6)
+    kv_far(kvf, fs_sem, fr_sem, 0)
+    kv_from_partner(kvf, fs_sem, fr_sem)
+    wo_take(1)
+    wo_take(7)
 
     inv_root = 1.0 / math.sqrt(DH)
-    lane = lax.broadcasted_iota(jnp.int32, (NZ * TOK, 128), 1)
-    ones = jnp.ones((NB * TOK, DH), BF16)
+    lane = lax.broadcasted_iota(jnp.int32, (NX * TOK, 128), 1)
+    ones = jnp.ones((NK * TOK, DH), BF16)
 
     def attend(s, held, own):
-        outs, stats = [], jnp.zeros((NZ * TOK, 128), F32)
+        outs, stats = [], jnp.zeros((NX * TOK, 128), F32)
         for i in range(2):
             cols = slice(i * DH, (i + 1) * DH)
-            keys = held[:, 0, :, cols].reshape(NB * TOK, DH)
-            vals = held[:, 1, :, cols].reshape(NB * TOK, DH)
+            keys = held[:, 0, :, cols].reshape(NK * TOK, DH)
+            vals = held[:, 1, :, cols].reshape(NK * TOK, DH)
             own_keys = jnp.concatenate([own[0, :, cols], keys[TOK:]], axis=0)
             own_vals = jnp.concatenate([own[1, :, cols], vals[TOK:]], axis=0)
-            q = qb[:, s * TOK : (s + 1) * TOK, cols].reshape(NZ * TOK, DH)
+            q = qb[:, s * TOK : (s + 1) * TOK, cols].reshape(NX * TOK, DH)
             scores = jnp.concatenate([dot_nt(q[:TOK], own_keys), dot_nt(q[TOK:], keys)], axis=0) * inv_root
             top = jnp.max(scores, axis=1, keepdims=True)
             weights = jnp.exp(scores - top).astype(BF16)
@@ -225,42 +268,39 @@
                 piece = left.astype(BF16).astype(F32)
                 stats = jnp.where(lane == 3 * i + k, piece, stats)
                 left = left - piece
-        full = jnp.concatenate(outs + [stats.astype(BF16)], axis=1).reshape(NZ, TOK, HC + 128)
+        full = jnp.concatenate(outs + [stats.astype(BF16)], axis=1).reshape(NX, TOK, HC + 128)
         orc[s, 0] = full[0]
-        for d in range(1, NZ):
+        for d in range(1, NX):
             os_[s, d] = full[d]
-        for d in (4, 3, 5, 2, 6, 1, 7):
-            send(os_.at[s, d], orc.at[s, NZ - d], os_sem.at[s, d], or_sem.at[s, NZ - d], z_peer(d))
-
+        for d in (2, 1, 3):
+            send(os_.at[s, d], orc.at[s, NX - d], os_sem.at[s, d], or_sem.at[s, NX - d], x_peer(d))
+
+    kv_all(kvs, ss_sem, sr_sem)
     for d in range(1, NX):
-        arrived(kvs.at[d], ss_sem.at[d], sr_sem.at[d], x_peer(d))
-        arrived(kvs.at[NX + d], ss_sem.at[NX + d], sr_sem.at[NX + d], x_peer(d))
-    for d in range(1, NZ):
-        arrived(qb.at[d], qs_sem.at[d], qr_sem.at[d], z_peer(d))
+        arrived(qb.at[d], qs_sem.at[d], qr_sem.at[d], x_peer(d))
     attend(0, kvs, kvf.at[0])
 
+    kv_far(kvf, fs_sem, fr_sem, 1)
     for d in (3, 5, 4):
-        forward_wo(d)
-
-    for d in range(1, NX):
-        arrived(kvf.at[d], fs_sem.at[d], fr_sem.at[d], x_peer(d))
-        arrived(kvf.at[NX + d], fs_sem.at[NX + d], fr_sem.at[NX + d], x_peer(d))
+        wo_take(d)
+
+    kv_all(kvf, fs_sem, fr_sem)
     attend(1, kvf, kv1)
 
     def merge(s):
-        for d in range(1, NZ):
-            arrived(orc.at[s, d], os_sem.at[s, d], or_sem.at[s, d], z_peer(d))
+        for d in range(1, NX):
+            arrived(orc.at[s, d], os_sem.at[s, d], or_sem.at[s, d], x_peer(d))
         heads = []
         for i in range(2):
             lse = []
-            for d in range(NZ):
+            for d in range(NX):
                 st = orc[s, d, :, HC : HC + 128].astype(F32)
                 k = 3 * i
                 lse.append(st[:, k : k + 1] + st[:, k + 1 : k + 2] + st[:, k + 2 : k + 3])
             top = functools.reduce(jnp.maximum, lse)
             mixed = jnp.zeros((TOK, DH), F32)
             total = jnp.zeros((TOK, 1), F32)
-            for d in range(NZ):
+            for d in range(NX):
                 weight = jnp.exp(lse[d] - top)
                 total += weight
                 mixed += weight * orc[s, d, :, i * DH : (i + 1) * DH].astype(F32)
@@ -328,12 +368,12 @@
             pltpu.VMEM((8, 2 * TOK, FEAT), BF16),
             pltpu.VMEM((8, 4, FEAT), F32),
             pltpu.VMEM((2 * TOK, WIDTH), BF16),
-            pltpu.VMEM((NB, 2, TOK, HC), BF16),
-            pltpu.VMEM((NB, 2, TOK, HC), BF16),
+            pltpu.VMEM((NK, 2, TOK, HC), BF16),
+            pltpu.VMEM((NK, 2, TOK, HC), BF16),
             pltpu.VMEM((2, TOK, HC), BF16),
-            pltpu.VMEM((NZ, 2 * TOK, HC), BF16),
-            pltpu.VMEM((2, NZ, TOK, HC + 128), BF16),
-            pltpu.VMEM((2, NZ, TOK, HC + 128), BF16),
+            pltpu.VMEM((NX, 2 * TOK, HC), BF16),
+            pltpu.VMEM((2, NX, TOK, HC + 128), BF16),
+            pltpu.VMEM((2, NX, TOK, HC + 128), BF16),
             pltpu.VMEM((NZ, NYH, NX, OUTC, HC), BF16),
             pltpu.VMEM((2, NYL, TOK, FEAT), BF16),
             pltpu.VMEM((2, NYL, TOK, FEAT), BF16),
@@ -342,9 +382,9 @@
             pltpu.VMEM((2, TOK, FEAT), F32),
             dma((5,)), dma((3,)),
             dma((7,)), dma((8,)), dma((7,)), dma((8,)),
-            dma((8,)), dma((8,)), dma((8,)), dma((8,)),
-            dma((8,)), dma((8,)), dma((2, 8)), dma((2, 8)),
-            dma, dma, dma((8,)), dma((8,)), dma((8, 4)), dma((4, 8)),
+            dma((18,)), dma((18,)), dma((18,)), dma((18,)),
+            dma((4,)), dma((4,)), dma((2, 4)), dma((2, 4)),
+            dma, dma, dma((8,)), dma((9,)), dma((8, 4)), dma((4, 8)),
             dma((2, 4)), dma((2, 4)), dma((2, 4)), dma((2, 4)),
         ],
         compiler_params=pltpu.CompilerParams(

time: 63.7 us -> 63.1 us (level)
  no operation moved by 1% of the time
where the time goes in v3:
time: 63.1 us; the launch traced here: 62.8 us
  Pallas kernels  59.9 us (95%)
  local copies, waits for them, and re-layouts  1.42 us (2%)
  other arithmetic  0.85 us (1%)
  between operations  0.68 us (1%)
    pallas_call x1, Pallas kernels, body(): pl.pallas_call(kernel, out_shape=jax.ShapeDtypeStruct((2 * TOK, FEAT), BF...  59.9 us
    unnamed x1, local copies, waits for them, and re-layouts  1.42 us

profile of v3, /device:TPU:1, one launch (start us, length us, event | category | flops | bytes accessed | tf_op | source)
XLA Modules:
  0.0 62.8 jit_solution(12385197103768878806)
XLA Ops:
  0.7 0.1 fusion
  0.8 0.7 %pad_maximum_fusion = (f32[32,128]{1,0:T(8,128)}, f32[32,128]{1,0:T(8,128)}) fusion(f32[32,64]{1,0:T(8,128)S(1)} %get-tuple-element.7, f32[32,64]{1,0:T(8,128)S(1)} %get-tuple-element.6, f32[32,64]{1,0:T(8,128)S(1)} %get-tuple-element.5), kind=kLoop, calls=%fused_computation.2 | loop fusion | flops 8192 | bytes 57344 | tf_op jit(solution)/shard_map/concatenate | solution.py:352
  1.5 59.9 %block.1 = bf16[64,384]{1,0:T(8,128)(2,1)} custom-call(bf16[64,384]{1,0:T(8,128)(2,1)} %bitcast.8, bf16[2,32,256]{2,1,0:T(8,128)(2,1)} %stale_ref.1, bf16[3,3072,256]{2,1,0:T(8,128)(2,1)} %bitcast.6, bf16[48,256]{1,0:T(8,128)(2,1)} %bitcast.9, f32[3,4,384]{2,1,0:T(4,128)} %bitcast.10, s32[2]{0:T(128)} %ids_ref.1, f32[32,128]{1,0:T(8,128)} %get-tuple-element.8.cos_ref, ...), custom_call_target="tpu_custom_call" | custom-call | tf_op jit(solution)/shard_map/block/pallas_call | solution.py:359
  61.4 1.4 %copy.10 = bf16[2,32,384]{2,1,0:T(8,128)(2,1)} copy(bf16[2,32,384]{2,1,0:T(8,128)(2,1)} %bitcast.7) | data formatting | bytes 98304
  (2 shorter events, 0.0 us)

commit v4 on v2

--- a/solution.py
+++ b/solution.py
@@ -31,9 +31,10 @@
 
 def kernel(
     x_ref, stale_ref, w_ref, wo_ref, mod_ref, ids_ref, cos_ref, sin_ref, out_ref,
-    ids_v, mod_v, w_v, xg, mg, a_v, kvs, kvf, kv1, qb, os_, orc, wo, e0s, e0r, e1s, e1r, acc,
+    ids_v, mod_v, w_v, xg, mg, a_v, kvs, kvf, kv1, qb, os_, orc, st, stc,
+    wo, e0s, e0r, e1s, e1r, acc,
     in_sem, w_sem, xs_sem, xr_sem, ms_sem, mr_sem,
-    ss_sem, sr_sem, fs_sem, fr_sem, qs_sem, qr_sem, os_sem, or_sem,
+    ss_sem, sr_sem, fs_sem, fr_sem, qs_sem, qr_sem, os_sem, or_sem, ts_sem, tr_sem,
     wys_sem, wyr_sem, wzs_sem, wzr_sem, wxs_sem, wxr_sem,
     e0s_sem, e0r_sem, e1s_sem, e1r_sem,
 ):
@@ -106,64 +107,54 @@
 
     pl.semaphore_wait(barrier, len(peers))
 
-    for d in (2, 1, 3):
-        send(xg.at[h], xg.at[h], xs_sem.at[d], xr_sem.at[h], y_peer(d))
-        send(mg.at[h], mg.at[h], ms_sem.at[d], mr_sem.at[h], y_peer(d))
-    send(xg.at[h], xg.at[h], xs_sem.at[0], xr_sem.at[h], sibling)
-    send(mg.at[h], mg.at[h], ms_sem.at[0], mr_sem.at[h], sibling)
+    for s in range(2):
+        for d in (2, 1, 3):
+            send(xg.at[h, s], xg.at[h, s], xs_sem.at[s, d], xr_sem.at[s, h], y_peer(d))
+            if s == 0:
+                send(mg.at[h], mg.at[h], ms_sem.at[d], mr_sem.at[h], y_peer(d))
+        send(xg.at[h, s], xg.at[h, s], xs_sem.at[s, 0], xr_sem.at[s, h], sibling)
+        if s == 0:
+            send(mg.at[h], mg.at[h], ms_sem.at[0], mr_sem.at[h], sibling)
+    for d in range(1, NX):
+        send(kvs.at[0], kvs.at[NX - d], ss_sem.at[d], sr_sem.at[NX - d], x_peer(d))
+    send(kvs.at[0], kvs.at[NX], ss_sem.at[0], sr_sem.at[NX], yh_peer)
     send(wo.at[z, yh, x], wo.at[z, yh, x], wys_sem, wyr_sem, yh_peer)
-    send(kvs.at[0], kvs.at[NX], ss_sem.at[0], sr_sem.at[NX], yh_peer)
-    for d in range(1, NX):
-        send(kvs.at[0], kvs.at[NX - d], ss_sem.at[d], sr_sem.at[NX - d], x_peer(d))
-
-    for d in range(1, NYL):
-        hs = ((yl + d) % NYL) * 2 + c
-        arrived(xg.at[hs], xs_sem.at[d], xr_sem.at[hs], y_peer(d))
-        arrived(mg.at[hs], ms_sem.at[d], mr_sem.at[hs], y_peer(d))
-        send(xg.at[hs], xg.at[hs], xs_sem.at[NYL - 1 + d], xr_sem.at[hs], sibling)
-        send(mg.at[hs], mg.at[hs], ms_sem.at[NYL - 1 + d], mr_sem.at[hs], sibling)
-
-    arrived(wo.at[z, 1 - yh, x], wys_sem, wyr_sem, yh_peer)
-    for d in (4, 3, 5, 2, 6, 1, 7):
-        send(wo.at[z, :, x], wo.at[z, :, x], wzs_sem.at[d], wzr_sem.at[z], z_peer(d))
-    arrived(kvs.at[NX], ss_sem.at[0], sr_sem.at[NX], yh_peer)
-    for d in range(1, NX):
-        send(kvs.at[NX], kvs.at[NX + NX - d], ss_sem.at[NX + d], sr_sem.at[NX + NX - d], x_peer(d))
-
-    for d in range(NYL):
-        hs = ((yl + d) % NYL) * 2 + 1 - c
-        arrived(xg.at[hs], xs_sem.at[0], xr_sem.at[hs], sibling)
-        arrived(mg.at[hs], ms_sem.at[0], mr_sem.at[hs], sibling)
-
-    def forward_wo(d):
-        zz = (z + d) % NZ
-        if d:
-            arrived(wo.at[zz, :, x], wzs_sem.at[d], wzr_sem.at[zz], z_peer(d))
-        for e in range(1, NX):
-            send(wo.at[zz, :, x], wo.at[zz, :, x], wxs_sem.at[d, e], wxr_sem.at[x, zz], x_peer(e))
-
-    forward_wo(0)
-
-    sum1 = jnp.zeros((2 * TOK, 128), F32)
-    sum2 = jnp.zeros((2 * TOK, 128), F32)
-    for j in range(8):
-        v = xg[j].astype(F32)
-        for k in range(FEAT // 128):
-            part = v[:, k * 128 : (k + 1) * 128]
-            sum1 += part
-            sum2 += part * part
-    mean = jnp.sum(sum1, axis=1, keepdims=True) / WIDTH
-    square = jnp.sum(sum2, axis=1, keepdims=True) / WIDTH
-    inv = lax.rsqrt(square - mean * mean + 1e-06)
-    for j in range(8):
-        v = (xg[j].astype(F32) - mean) * inv
-        m = mg[j]
-        for s in range(2):
-            part = v[s * TOK : (s + 1) * TOK] * (1.0 + m[2 + s : 3 + s]) + m[s : s + 1]
-            a_v[s * TOK : (s + 1) * TOK, j * FEAT : (j + 1) * FEAT] = part.astype(BF16)
-
-    cos = jnp.concatenate([cos_ref[...]] * 2, axis=0)
-    sin = jnp.concatenate([sin_ref[...]] * 2, axis=0)
+
+    def rows_forward(s):
+        for d in (1, 3, 2):
+            hs = ((yl + d) % NYL) * 2 + c
+            arrived(xg.at[hs, s], xs_sem.at[s, d], xr_sem.at[s, hs], y_peer(d))
+            send(xg.at[hs, s], xg.at[hs, s], xs_sem.at[s, NYL - 1 + d], xr_sem.at[s, hs], sibling)
+            if s == 0:
+                arrived(mg.at[hs], ms_sem.at[d], mr_sem.at[hs], y_peer(d))
+                send(mg.at[hs], mg.at[hs], ms_sem.at[NYL - 1 + d], mr_sem.at[hs], sibling)
+
+    def rows_done(s):
+        for d in range(NYL):
+            hs = ((yl + d) % NYL) * 2 + 1 - c
+            arrived(xg.at[hs, s], xs_sem.at[s, 0], xr_sem.at[s, hs], sibling)
+            if s == 0:
+                arrived(mg.at[hs], ms_sem.at[0], mr_sem.at[hs], sibling)
+
+    def normalize(s):
+        sum1 = jnp.zeros((TOK, 128), F32)
+        sum2 = jnp.zeros((TOK, 128), F32)
+        for j in range(8):
+            v = xg[j, s].astype(F32)
+            for k in range(FEAT // 128):
+                part = v[:, k * 128 : (k + 1) * 128]
+                sum1 += part
+                sum2 += part * part
+        mean = jnp.sum(sum1, axis=1, keepdims=True) / WIDTH
+        square = jnp.sum(sum2, axis=1, keepdims=True) / WIDTH
+        inv = lax.rsqrt(square - mean * mean + 1e-06)
+        for j in range(8):
+            v = (xg[j, s].astype(F32) - mean) * inv
+            v = v * (1.0 + mg[j, 2 + s : 3 + s]) + mg[j, s : s + 1]
+            a_v[s, :, j * FEAT : (j + 1) * FEAT] = v.astype(BF16)
+
+    cos = cos_ref[...]
+    sin = sin_ref[...]
 
     def rot(u):
         heads = []
@@ -172,42 +163,71 @@
             heads.append(uh * cos + pltpu.roll(uh, DH // 2, 1) * sin)
         return jnp.concatenate(heads, axis=1).astype(BF16)
 
-    loads[1].wait()
-    kr = rot(dot_nn(a_v[...], w_v[1]))
-    loads[2].wait()
-    vr = dot_nn(a_v[...], w_v[2]).astype(BF16)
-    kvf[0, 0] = kr[:TOK]
-    kvf[0, 1] = vr[:TOK]
-    kv1[0] = kr[TOK:]
-    kv1[1] = vr[TOK:]
+    def project_in(s, own):
+        if s == 0:
+            loads[1].wait()
+        own[0] = rot(dot_nn(a_v[s], w_v[1]))
+        if s == 0:
+            loads[2].wait()
+        own[1] = dot_nn(a_v[s], w_v[2]).astype(BF16)
+
+    def queries(s):
+        if s == 0:
+            loads[0].wait()
+        qb[0, s] = rot(dot_nn(a_v[s], w_v[0]))
+        for d in (4, 3, 5, 2, 6, 1, 7):
+            send(qb.at[0, s], qb.at[NZ - d, s], qs_sem.at[s, d], qr_sem.at[s, NZ - d], z_peer(d))
+
+    def forward_wo(d):
+        zz = (z + d) % NZ
+        if d:
+            arrived(wo.at[zz, :, x], wzs_sem.at[d], wzr_sem.at[zz], z_peer(d))
+        for e in (2, 1, 3):
+            send(wo.at[zz, :, x], wo.at[zz, :, x], wxs_sem.at[d, e], wxr_sem.at[x, zz], x_peer(e))
+
+    rows_forward(0)
+    rows_done(0)
+    normalize(0)
+    project_in(0, kvf.at[0])
     send(kvf.at[0], kvf.at[NX], fs_sem.at[0], fr_sem.at[NX], yh_peer)
     for d in range(1, NX):
         send(kvf.at[0], kvf.at[NX - d], fs_sem.at[d], fr_sem.at[NX - d], x_peer(d))
-    loads[0].wait()
-    qb[0] = rot(dot_nn(a_v[...], w_v[0]))
-    for d in (4, 3, 5, 2, 6, 1, 7):
-        send(qb.at[0], qb.at[NZ - d], qs_sem.at[d], qr_sem.at[NZ - d], z_peer(d))
-
+    rows_forward(1)
+    queries(0)
+
+    arrived(kvs.at[NX], ss_sem.at[0], sr_sem.at[NX], yh_peer)
+    for d in range(1, NX):
+        send(kvs.at[NX], kvs.at[NX + NX - d], ss_sem.at[NX + d], sr_sem.at[NX + NX - d], x_peer(d))
+    arrived(wo.at[z, 1 - yh, x], wys_sem, wyr_sem, yh_peer)
+    for d in (1, 7, 2, 6, 3, 5, 4):
+        send(wo.at[z, :, x], wo.at[z, :, x], wzs_sem.at[d], wzr_sem.at[z], z_peer(d))
+    forward_wo(0)
+
+    rows_done(1)
+    normalize(1)
+    queries(1)
+    project_in(1, kv1)
+
+    for d in (1, 7):
+        forward_wo(d)
     arrived(kvf.at[NX], fs_sem.at[0], fr_sem.at[NX], yh_peer)
     for d in range(1, NX):
         send(kvf.at[NX], kvf.at[NX + NX - d], fs_sem.at[NX + d], fr_sem.at[NX + NX - d], x_peer(d))
-
-    for d in (1, 7, 2, 6):
+    for d in (2, 6):
         forward_wo(d)
 
     inv_root = 1.0 / math.sqrt(DH)
-    lane = lax.broadcasted_iota(jnp.int32, (NZ * TOK, 128), 1)
     ones = jnp.ones((NB * TOK, DH), BF16)
+    diagonal = lax.broadcasted_iota(jnp.int32, (128, 128), 0) == lax.broadcasted_iota(jnp.int32, (128, 128), 1)
 
     def attend(s, held, own):
-        outs, stats = [], jnp.zeros((NZ * TOK, 128), F32)
         for i in range(2):
             cols = slice(i * DH, (i + 1) * DH)
             keys = held[:, 0, :, cols].reshape(NB * TOK, DH)
             vals = held[:, 1, :, cols].reshape(NB * TOK, DH)
             own_keys = jnp.concatenate([own[0, :, cols], keys[TOK:]], axis=0)
             own_vals = jnp.concatenate([own[1, :, cols], vals[TOK:]], axis=0)
-            q = qb[:, s * TOK : (s + 1) * TOK, cols].reshape(NZ * TOK, DH)
+            q = qb[:, s, :, cols].reshape(NZ * TOK, DH)
             scores = jnp.concatenate([dot_nt(q[:TOK], own_keys), dot_nt(q[TOK:], keys)], axis=0) * inv_root
             top = jnp.max(scores, axis=1, keepdims=True)
             weights = jnp.exp(scores - top).astype(BF16)
@@ -219,24 +239,21 @@
                 axis=0,
             )
             total = mixed[:, DH:]
-            outs.append((mixed[:, :DH] / total).astype(BF16))
-            left = top + jnp.log(total)
-            for k in range(3):
-                piece = left.astype(BF16).astype(F32)
-                stats = jnp.where(lane == 3 * i + k, piece, stats)
-                left = left - piece
-        full = jnp.concatenate(outs + [stats.astype(BF16)], axis=1).reshape(NZ, TOK, HC + 128)
-        orc[s, 0] = full[0]
-        for d in range(1, NZ):
-            os_[s, d] = full[d]
+            os_[s, :, :, cols] = (mixed[:, :DH] / total).astype(BF16).reshape(NZ, TOK, DH)
+            lse = top + jnp.log(total)
+            for k in range(NZ * TOK // 128):
+                part = lse[k * 128 : (k + 1) * 128]
+                row = jnp.sum(jnp.where(diagonal, part, 0.0), axis=0, keepdims=True)
+                st[s, i : i + 1, k * 128 : (k + 1) * 128] = row
         for d in (4, 3, 5, 2, 6, 1, 7):
             send(os_.at[s, d], orc.at[s, NZ - d], os_sem.at[s, d], or_sem.at[s, NZ - d], z_peer(d))
+            send(st.at[s], stc.at[s, NZ - d], ts_sem.at[s, d], tr_sem.at[s, NZ - d], z_peer(d))
 
     for d in range(1, NX):
         arrived(kvs.at[d], ss_sem.at[d], sr_sem.at[d], x_peer(d))
         arrived(kvs.at[NX + d], ss_sem.at[NX + d], sr_sem.at[NX + d], x_peer(d))
     for d in range(1, NZ):
-        arrived(qb.at[d], qs_sem.at[d], qr_sem.at[d], z_peer(d))
+        arrived(qb.at[d, 0], qs_sem.at[0, d], qr_sem.at[0, d], z_peer(d))
     attend(0, kvs, kvf.at[0])
 
     for d in (3, 5, 4):
@@ -245,25 +262,33 @@
     for d in range(1, NX):
         arrived(kvf.at[d], fs_sem.at[d], fr_sem.at[d], x_peer(d))
         arrived(kvf.at[NX + d], fs_sem.at[NX + d], fr_sem.at[NX + d], x_peer(d))
+    for d in range(1, NZ):
+        arrived(qb.at[d, 1], qs_sem.at[1, d], qr_sem.at[1, d], z_peer(d))
     attend(1, kvf, kv1)
+
+    row_id = lax.broadcasted_iota(jnp.int32, (TOK, 128), 0)
+    lane_id = lax.broadcasted_iota(jnp.int32, (TOK, 128), 1)
 
     def merge(s):
         for d in range(1, NZ):
             arrived(orc.at[s, d], os_sem.at[s, d], or_sem.at[s, d], z_peer(d))
+            arrived(stc.at[s, d], ts_sem.at[s, d], tr_sem.at[s, d], z_peer(d))
         heads = []
         for i in range(2):
             lse = []
             for d in range(NZ):
-                st = orc[s, d, :, HC : HC + 128].astype(F32)
-                k = 3 * i
-                lse.append(st[:, k : k + 1] + st[:, k + 1 : k + 2] + st[:, k + 2 : k + 3])
+                held = st if d == 0 else stc.at[:, d]
+                at = (NZ - d) % NZ * TOK
+                row = held[s, i : i + 1, at // 128 * 128 : at // 128 * 128 + 128]
+                lse.append(jnp.sum(jnp.where(lane_id == row_id + at % 128, row, 0.0), axis=1, keepdims=True))
             top = functools.reduce(jnp.maximum, lse)
             mixed = jnp.zeros((TOK, DH), F32)
             total = jnp.zeros((TOK, 1), F32)
             for d in range(NZ):
                 weight = jnp.exp(lse[d] - top)
                 total += weight
-                mixed += weight * orc[s, d, :, i * DH : (i + 1) * DH].astype(F32)
+                part = (os_ if d == 0 else orc)[s, d, :, i * DH : (i + 1) * DH]
+                mixed += weight * part.astype(F32)
             heads.append((mixed / total).astype(BF16))
         return jnp.concatenate(heads, axis=1)
 
@@ -325,15 +350,17 @@
             pltpu.SMEM((2,), jnp.int32),
             pltpu.VMEM((3, 4, FEAT), F32),
             pltpu.VMEM((3, WIDTH, HC), BF16),
-            pltpu.VMEM((8, 2 * TOK, FEAT), BF16),
+            pltpu.VMEM((8, 2, TOK, FEAT), BF16),
             pltpu.VMEM((8, 4, FEAT), F32),
-            pltpu.VMEM((2 * TOK, WIDTH), BF16),
+            pltpu.VMEM((2, TOK, WIDTH), BF16),
             pltpu.VMEM((NB, 2, TOK, HC), BF16),
             pltpu.VMEM((NB, 2, TOK, HC), BF16),
             pltpu.VMEM((2, TOK, HC), BF16),
-            pltpu.VMEM((NZ, 2 * TOK, HC), BF16),
-            pltpu.VMEM((2, NZ, TOK, HC + 128), BF16),
-            pltpu.VMEM((2, NZ, TOK, HC + 128), BF16),
+            pltpu.VMEM((NZ, 2, TOK, HC), BF16),
+            pltpu.VMEM((2, NZ, TOK, HC), BF16),
+            pltpu.VMEM((2, NZ, TOK, HC), BF16),
+            pltpu.VMEM((2, 2, NZ * TOK), F32),
+            pltpu.VMEM((2, NZ, 2, NZ * TOK), F32),
             pltpu.VMEM((NZ, NYH, NX, OUTC, HC), BF16),
             pltpu.VMEM((2, NYL, TOK, FEAT), BF16),
             pltpu.VMEM((2, NYL, TOK, FEAT), BF16),
@@ -341,9 +368,9 @@
             pltpu.VMEM((2, NYL, TOK, FEAT), BF16),
             pltpu.VMEM((2, TOK, FEAT), F32),
             dma((5,)), dma((3,)),
-            dma((7,)), dma((8,)), dma((7,)), dma((8,)),
+            dma((2, 7)), dma((2, 8)), dma((7,)), dma((8,)),
             dma((8,)), dma((8,)), dma((8,)), dma((8,)),
-            dma((8,)), dma((8,)), dma((2, 8)), dma((2, 8)),
+            dma((2, 8)), dma((2, 8)), dma((2, 8)), dma((2, 8)), dma((2, 8)), dma((2, 8)),
             dma, dma, dma((8,)), dma((8,)), dma((8, 4)), dma((4, 8)),
             dma((2, 4)), dma((2, 4)), dma((2, 4)), dma((2, 4)),
         ],
@@ -352,7 +379,7 @@
         ),
         name="block",
     )(
-        inputs.reshape(2 * TOK, FEAT),
+        inputs,
         stale_kv,
         jnp.transpose(w_qkv, (1, 0, 2)),
         jnp.transpose(w_out),

time: 63.7 us -> 63.7 us (level)
  no operation moved by 1% of the time
where the time goes in v4:
time: 63.7 us; the launch traced here: 63.5 us
  Pallas kernels  60.5 us (95%)
  local copies, waits for them, and re-layouts  1.42 us (2%)
  other arithmetic  0.85 us (1%)
  between operations  0.68 us (1%)
    pallas_call x1, Pallas kernels, body(): pl.pallas_call(kernel, out_shape=jax.ShapeDtypeStruct((2 * TOK, FEAT), BF...  60.5 us
    unnamed x1, local copies, waits for them, and re-layouts  1.42 us

profile of v4, /device:TPU:1, one launch (start us, length us, event | category | flops | bytes accessed | tf_op | source)
XLA Modules:
  0.0 63.5 jit_solution(15974837539932724249)
XLA Ops:
  0.7 0.1 fusion
  0.8 0.7 %pad_maximum_fusion = (f32[32,128]{1,0:T(8,128)}, f32[32,128]{1,0:T(8,128)}) fusion(f32[32,64]{1,0:T(8,128)S(1)} %get-tuple-element.7, f32[32,64]{1,0:T(8,128)S(1)} %get-tuple-element.6, f32[32,64]{1,0:T(8,128)S(1)} %get-tuple-element.5), kind=kLoop, calls=%fused_computation.2 | loop fusion | flops 8192 | bytes 57344 | tf_op jit(solution)/shard_map/concatenate | solution.py:337
  1.5 60.5 %block.1 = bf16[64,384]{1,0:T(8,128)(2,1)} custom-call(bf16[2,32,384]{2,1,0:T(8,128)(2,1)} %x_ref.1, bf16[2,32,256]{2,1,0:T(8,128)(2,1)} %stale_ref.1, bf16[3,3072,256]{2,1,0:T(8,128)(2,1)} %bitcast.5, bf16[48,256]{1,0:T(8,128)(2,1)} %bitcast.7, f32[3,4,384]{2,1,0:T(4,128)} %bitcast.8, s32[2]{0:T(128)} %ids_ref.1, f32[32,128]{1,0:T(8,128)} %get-tuple-element.8.cos_ref, ...), custom_call_target="tpu_custom_call" | custom-call | tf_op jit(solution)/shard_map/block/pallas_call | solution.py:344
  62.0 1.4 %copy.10 = bf16[2,32,384]{2,1,0:T(8,128)(2,1)} copy(bf16[2,32,384]{2,1,0:T(8,128)(2,1)} %bitcast.6) | data formatting | bytes 98304
  (2 shorter events, 0.0 us)

commit v5 on v4

--- a/solution.py
+++ b/solution.py
@@ -16,6 +16,7 @@
 OUTC = 48
 NZ, NYH, NX, NYL = 8, 2, 4, 4
 NB = NYH * NX
+RELAY = frozenset([(0, 0), (0, 1), (0, 2), (0, 3), (0, 4), (0, 5), (0, 6), (0, 7), (1, 0), (1, 1), (1, 2), (1, 3), (1, 4), (1, 5), (1, 6), (1, 7)])
 F32 = jnp.float32
 BF16 = jnp.bfloat16
 MESH = pl.DeviceIdType.MESH
@@ -107,6 +108,34 @@
 
     pl.semaphore_wait(barrier, len(peers))
 
+    def wo_block(plane, dz, dx=0):
+        return wo.at[(z + dz) % NZ, yh if plane == 0 else 1 - yh, (x + dx) % NX]
+
+    relayed = set()
+
+    def wo_along_x(plane, d):
+        piece = wo_block(plane, d)
+        for e in (1, 3) if (plane, d) in RELAY else (2, 1, 3):
+            send(piece, piece, wxs_sem.at[plane, d, e], wxr_sem.at[plane, (NX - e) % NX, d], x_peer(e))
+
+    def wo_relay(plane, d):
+        e = 3 if plane == 0 else 1
+        piece = wo_block(plane, d, e)
+        arrived(piece, wxs_sem.at[plane, d, e], wxr_sem.at[plane, e, d], x_peer(e))
+        send(piece, piece, wxs_sem.at[plane, d, 2], wxr_sem.at[plane, 2, d], x_peer(NX - e))
+        relayed.add((plane, d, e))
+
+    def wo_start(plane):
+        piece = wo_block(plane, 0)
+        for d in (1, 7, 2, 6, 3, 5, 4):
+            send(piece, piece, wzs_sem.at[plane, d], wzr_sem.at[plane, NZ - d], z_peer(d))
+        wo_along_x(plane, 0)
+
+    def wo_forward(plane, d):
+        arrived(wo_block(plane, d), wzs_sem.at[plane, d], wzr_sem.at[plane, d], z_peer(d))
+        wo_along_x(plane, d)
+
+    send(wo_block(0, 0), wo_block(0, 0), wys_sem, wyr_sem, yh_peer)
     for s in range(2):
         for d in (2, 1, 3):
             send(xg.at[h, s], xg.at[h, s], xs_sem.at[s, d], xr_sem.at[s, h], y_peer(d))
@@ -115,10 +144,10 @@
         send(xg.at[h, s], xg.at[h, s], xs_sem.at[s, 0], xr_sem.at[s, h], sibling)
         if s == 0:
             send(mg.at[h], mg.at[h], ms_sem.at[0], mr_sem.at[h], sibling)
+    wo_start(0)
     for d in range(1, NX):
         send(kvs.at[0], kvs.at[NX - d], ss_sem.at[d], sr_sem.at[NX - d], x_peer(d))
     send(kvs.at[0], kvs.at[NX], ss_sem.at[0], sr_sem.at[NX], yh_peer)
-    send(wo.at[z, yh, x], wo.at[z, yh, x], wys_sem, wyr_sem, yh_peer)
 
     def rows_forward(s):
         for d in (1, 3, 2):
@@ -178,14 +207,9 @@
         for d in (4, 3, 5, 2, 6, 1, 7):
             send(qb.at[0, s], qb.at[NZ - d, s], qs_sem.at[s, d], qr_sem.at[s, NZ - d], z_peer(d))
 
-    def forward_wo(d):
-        zz = (z + d) % NZ
-        if d:
-            arrived(wo.at[zz, :, x], wzs_sem.at[d], wzr_sem.at[zz], z_peer(d))
-        for e in (2, 1, 3):
-            send(wo.at[zz, :, x], wo.at[zz, :, x], wxs_sem.at[d, e], wxr_sem.at[x, zz], x_peer(e))
-
     rows_forward(0)
+    arrived(wo_block(1, 0), wys_sem, wyr_sem, yh_peer)
+    wo_start(1)
     rows_done(0)
     normalize(0)
     project_in(0, kvf.at[0])
@@ -198,23 +222,27 @@
     arrived(kvs.at[NX], ss_sem.at[0], sr_sem.at[NX], yh_peer)
     for d in range(1, NX):
         send(kvs.at[NX], kvs.at[NX + NX - d], ss_sem.at[NX + d], sr_sem.at[NX + NX - d], x_peer(d))
-    arrived(wo.at[z, 1 - yh, x], wys_sem, wyr_sem, yh_peer)
-    for d in (1, 7, 2, 6, 3, 5, 4):
-        send(wo.at[z, :, x], wo.at[z, :, x], wzs_sem.at[d], wzr_sem.at[z], z_peer(d))
-    forward_wo(0)
+    for d in (1, 7, 2, 6):
+        wo_forward(0, d)
 
     rows_done(1)
     normalize(1)
     queries(1)
     project_in(1, kv1)
-
-    for d in (1, 7):
-        forward_wo(d)
+    for d in (0,):
+        wo_relay(0, d)
+
+    for d in (3, 5, 4):
+        wo_forward(0, d)
     arrived(kvf.at[NX], fs_sem.at[0], fr_sem.at[NX], yh_peer)
     for d in range(1, NX):
         send(kvf.at[NX], kvf.at[NX + NX - d], fs_sem.at[NX + d], fr_sem.at[NX + NX - d], x_peer(d))
-    for d in (2, 6):
-        forward_wo(d)
+    for d in (1, 7, 2, 6):
+        wo_forward(1, d)
+    for d in (1, 7, 2, 6,):
+        wo_relay(0, d)
+    for d in (0,):
+        wo_relay(1, d)
 
     inv_root = 1.0 / math.sqrt(DH)
     ones = jnp.ones((NB * TOK, DH), BF16)
@@ -255,9 +283,11 @@
     for d in range(1, NZ):
         arrived(qb.at[d, 0], qs_sem.at[0, d], qr_sem.at[0, d], z_peer(d))
     attend(0, kvs, kvf.at[0])
-
     for d in (3, 5, 4):
-        forward_wo(d)
+        wo_forward(1, d)
+    for d in (3, 5, 4,):
+        wo_relay(0, d)
+
 
     for d in range(1, NX):
         arrived(kvf.at[d], fs_sem.at[d], fr_sem.at[d], x_peer(d))
@@ -265,6 +295,8 @@
     for d in range(1, NZ):
         arrived(qb.at[d, 1], qs_sem.at[1, d], qr_sem.at[1, d], z_peer(d))
     attend(1, kvf, kv1)
+    for d in (1, 7, 2, 6, 3, 5, 4,):
+        wo_relay(1, d)
 
     row_id = lax.broadcasted_iota(jnp.int32, (TOK, 128), 0)
     lane_id = lax.broadcasted_iota(jnp.int32, (TOK, 128), 1)
@@ -299,9 +331,11 @@
         o = merge(s)
         if s == 0:
             for e in range(1, NX):
-                for zz in range(NZ):
-                    xs = (x + e) % NX
-                    arrived(wo.at[zz, :, xs], wxs_sem.at[0, e], wxr_sem.at[xs, zz], x_peer(e))
+                for d in range(NZ):
+                    for plane in range(NYH):
+                        if (plane, d, e) in relayed:
+                            continue
+                        arrived(wo_block(plane, d, e), wxs_sem.at[plane, d, e], wxr_sem.at[plane, e, d], x_peer(e))
         for j in (2, 1, 3, 0):
             e0s[s, j] = block(o, j, 1 - c).astype(BF16)
             send(e0s.at[s, j], e0r.at[s, j], e0s_sem.at[s, j], e0r_sem.at[s, j], sibling)
@@ -371,7 +405,7 @@
             dma((2, 7)), dma((2, 8)), dma((7,)), dma((8,)),
             dma((8,)), dma((8,)), dma((8,)), dma((8,)),
             dma((2, 8)), dma((2, 8)), dma((2, 8)), dma((2, 8)), dma((2, 8)), dma((2, 8)),
-            dma, dma, dma((8,)), dma((8,)), dma((8, 4)), dma((4, 8)),
+            dma, dma, dma((2, 8)), dma((2, 8)), dma((2, 8, 4)), dma((2, 4, 8)),
             dma((2, 4)), dma((2, 4)), dma((2, 4)), dma((2, 4)),
         ],
         compiler_params=pltpu.CompilerParams(

time: 63.7 us -> 55.9 us (0.88)
  Pallas kernels: 60.5 us -> 52.7 us
    pallas_call x1, Pallas kernels: 60.5 us -> 52.7 us  [body(): pl.pallas_call(kernel, out_shape=jax.ShapeDtypeStruct((2 * TOK, FEAT), BF...]
where the time goes in v5:
time: 55.9 us; the launch traced here: 55.6 us
  Pallas kernels  52.7 us (94%)
  local copies, waits for them, and re-layouts  1.42 us (3%)
  other arithmetic  0.85 us (2%)
  between operations  0.68 us (1%)
    pallas_call x1, Pallas kernels, body(): pl.pallas_call(kernel, out_shape=jax.ShapeDtypeStruct((2 * TOK, FEAT), BF...  52.7 us
    unnamed x1, local copies, waits for them, and re-layouts  1.42 us

profile of v5, /device:TPU:1, one launch (start us, length us, event | category | flops | bytes accessed | tf_op | source)
XLA Modules:
  0.0 55.6 jit_solution(1545891577112992900)
XLA Ops:
  0.7 0.1 fusion
  0.8 0.7 %pad_maximum_fusion = (f32[32,128]{1,0:T(8,128)}, f32[32,128]{1,0:T(8,128)}) fusion(f32[32,64]{1,0:T(8,128)S(1)} %get-tuple-element.7, f32[32,64]{1,0:T(8,128)S(1)} %get-tuple-element.6, f32[32,64]{1,0:T(8,128)S(1)} %get-tuple-element.5), kind=kLoop, calls=%fused_computation.2 | loop fusion | flops 8192 | bytes 57344 | tf_op jit(solution)/shard_map/concatenate | solution.py:371
  1.5 52.7 %block.1 = bf16[64,384]{1,0:T(8,128)(2,1)} custom-call(bf16[2,32,384]{2,1,0:T(8,128)(2,1)} %x_ref.1, bf16[2,32,256]{2,1,0:T(8,128)(2,1)} %stale_ref.1, bf16[3,3072,256]{2,1,0:T(8,128)(2,1)} %bitcast.5, bf16[48,256]{1,0:T(8,128)(2,1)} %bitcast.7, f32[3,4,384]{2,1,0:T(4,128)} %bitcast.8, s32[2]{0:T(128)} %ids_ref.1, f32[32,128]{1,0:T(8,128)} %get-tuple-element.8.cos_ref, ...), custom_call_target="tpu_custom_call" | custom-call | tf_op jit(solution)/shard_map/block/pallas_call | solution.py:378
  54.2 1.4 %copy.10 = bf16[2,32,384]{2,1,0:T(8,128)(2,1)} copy(bf16[2,32,384]{2,1,0:T(8,128)(2,1)} %bitcast.6) | data formatting | bytes 98304
  (2 shorter events, 0.0 us)

commit v6 on v5

--- a/solution.py
+++ b/solution.py
@@ -31,8 +31,8 @@
 
 
 def kernel(
-    x_ref, stale_ref, w_ref, wo_ref, mod_ref, ids_ref, cos_ref, sin_ref, out_ref,
-    ids_v, mod_v, w_v, xg, mg, a_v, kvs, kvf, kv1, qb, os_, orc, st, stc,
+    x_ref, stale_ref, w_ref, wo_ref, mod_ref, ids_ref, order_ref, out_ref,
+    ids_v, order_v, mod_v, w_v, xg, mg, a_v, kvs, kvf, kv1, qb, os_, orc, st, stc,
     wo, e0s, e0r, e1s, e1r, acc,
     in_sem, w_sem, xs_sem, xr_sem, ms_sem, mr_sem,
     ss_sem, sr_sem, fs_sem, fr_sem, qs_sem, qr_sem, os_sem, or_sem, ts_sem, tr_sem,
@@ -82,6 +82,7 @@
 
     small = [
         pltpu.make_async_copy(ids_ref, ids_v, in_sem.at[0]),
+        pltpu.make_async_copy(order_ref, order_v, in_sem.at[5]),
         pltpu.make_async_copy(mod_ref, mod_v, in_sem.at[1]),
         pltpu.make_async_copy(x_ref, xg.at[h], in_sem.at[2]),
         pltpu.make_async_copy(stale_ref, kvs.at[0], in_sem.at[3]),
@@ -92,8 +93,8 @@
     loads = [pltpu.make_async_copy(w_ref.at[t], w_v.at[t], w_sem.at[t]) for t in range(3)]
     for t in (1, 2, 0):
         loads[t].start()
-    small[0].wait()
-    small[1].wait()
+    for load in small[:3]:
+        load.wait()
 
     table_row = lax.broadcasted_iota(jnp.int32, (4, FEAT), 0)
     gates = []
@@ -103,7 +104,14 @@
         mg[h, s : s + 1] = rows[0]
         mg[h, 2 + s : 3 + s] = rows[1]
         gates.append(rows[2])
-    for load in small[2:]:
+    token = lax.broadcasted_iota(jnp.int32, (TOK, DH), 0)
+    lane = lax.broadcasted_iota(jnp.int32, (TOK, DH), 1)
+    half = DH // 2
+    exponent = jnp.where(lane < half, lane, lane - half).astype(F32) * (-math.log(10000.0) / half)
+    angle = (order_v[0] * TOK + token).astype(F32) * jnp.exp(exponent)
+    cos = jnp.cos(angle)
+    sin = jnp.where(lane < half, -1.0, 1.0) * jnp.sin(angle)
+    for load in small[3:]:
         load.wait()
 
     pl.semaphore_wait(barrier, len(peers))
@@ -181,9 +189,6 @@
             v = (xg[j, s].astype(F32) - mean) * inv
             v = v * (1.0 + mg[j, 2 + s : 3 + s]) + mg[j, s : s + 1]
             a_v[s, :, j * FEAT : (j + 1) * FEAT] = v.astype(BF16)
-
-    cos = cos_ref[...]
-    sin = sin_ref[...]
 
     def rot(u):
         heads = []
@@ -362,26 +367,17 @@
         copy.wait_send()
 
 
-def tables(slab_order):
-    positions = slab_order[0] * TOK + jnp.arange(TOK, dtype=jnp.int32)
-    half = DH // 2
-    frequency = 10000.0 ** (-(2.0 * jnp.arange(half, dtype=F32)) / DH)
-    angle = positions.astype(F32)[:, None] * frequency[None, :]
-    cos, sin = jnp.cos(angle), jnp.sin(angle)
-    return jnp.concatenate([cos, cos], axis=1), jnp.concatenate([-sin, sin], axis=1)
-
-
 def body(inputs, stale_kv, w_qkv, w_out, mod_table, step_ids, slab_order):
-    cos, sin = tables(slab_order)
     vmem = pl.BlockSpec(memory_space=pltpu.VMEM)
     dma = pltpu.SemaphoreType.DMA
     out = pl.pallas_call(
         kernel,
         out_shape=jax.ShapeDtypeStruct((2 * TOK, FEAT), BF16),
-        in_specs=[pl.BlockSpec(memory_space=pltpu.HBM)] * 6 + [vmem] * 2,
+        in_specs=[pl.BlockSpec(memory_space=pltpu.HBM)] * 7,
         out_specs=vmem,
         scratch_shapes=[
             pltpu.SMEM((2,), jnp.int32),
+            pltpu.SMEM((1,), jnp.int32),
             pltpu.VMEM((3, 4, FEAT), F32),
             pltpu.VMEM((3, WIDTH, HC), BF16),
             pltpu.VMEM((8, 2, TOK, FEAT), BF16),
@@ -401,7 +397,7 @@
             pltpu.VMEM((2, NYL, TOK, FEAT), BF16),
             pltpu.VMEM((2, NYL, TOK, FEAT), BF16),
             pltpu.VMEM((2, TOK, FEAT), F32),
-            dma((5,)), dma((3,)),
+            dma((6,)), dma((3,)),
             dma((2, 7)), dma((2, 8)), dma((7,)), dma((8,)),
             dma((8,)), dma((8,)), dma((8,)), dma((8,)),
             dma((2, 8)), dma((2, 8)), dma((2, 8)), dma((2, 8)), dma((2, 8)), dma((2, 8)),
@@ -419,8 +415,7 @@
         jnp.transpose(w_out),
         jnp.transpose(mod_table, (1, 0, 2)),
         step_ids,
-        cos,
-        sin,
+        slab_order,
     )
     return out.reshape(2, TOK, FEAT)
 

time: 55.9 us -> 54.3 us (0.971)
  other arithmetic: 0.85 us -> 0 us
  Pallas kernels: 52.7 us -> 52 us
    concatenate x1 -> x0, other arithmetic: 0.69 us -> none  [tables(): jnp.concatenate([cos, cos], axis=1)]
    pallas_call x1, Pallas kernels: 52.7 us -> 52 us  [body(): pl.pallas_call(kernel, out_shape=jax.ShapeDtypeStruct((2 * TOK, FEAT), BF...]
where the time goes in v6:
time: 54.3 us; the launch traced here: 54.1 us
  Pallas kernels  52 us (96%)
  local copies, waits for them, and re-layouts  1.42 us (3%)
  between operations  0.66 us (1%)
    pallas_call x1, Pallas kernels, body(): pl.pallas_call(kernel, out_shape=jax.ShapeDtypeStruct((2 * TOK, FEAT), BF...  52 us
    unnamed x1, local copies, waits for them, and re-layouts  1.42 us

profile of v6, /device:TPU:1, one launch (start us, length us, event | category | flops | bytes accessed | tf_op | source)
XLA Modules:
  0.0 54.1 jit_solution(6246352222019810864)
XLA Ops:
  0.7 52.0 %block.1 = bf16[64,384]{1,0:T(8,128)(2,1)} custom-call(bf16[2,32,384]{2,1,0:T(8,128)(2,1)} %x_ref.1, bf16[2,32,256]{2,1,0:T(8,128)(2,1)} %stale_ref.1, bf16[3,3072,256]{2,1,0:T(8,128)(2,1)} %bitcast.4, bf16[48,256]{1,0:T(8,128)(2,1)} %bitcast.6, f32[3,4,384]{2,1,0:T(4,128)} %bitcast.7, s32[2]{0:T(128)} %ids_ref.1, s32[1]{0:T(128)S(6)} %copy.9.order_ref), custom_call_target="tpu_custom_call" | custom-call | tf_op jit(solution)/shard_map/block/pallas_call | solution.py:373
  52.7 1.4 %copy.10 = bf16[2,32,384]{2,1,0:T(8,128)(2,1)} copy(bf16[2,32,384]{2,1,0:T(8,128)(2,1)} %bitcast.5) | data formatting | bytes 98304

commit v7 on v6

--- a/solution.py
+++ b/solution.py
@@ -299,6 +299,7 @@
         arrived(kvf.at[NX + d], fs_sem.at[NX + d], fr_sem.at[NX + d], x_peer(d))
     for d in range(1, NZ):
         arrived(qb.at[d, 1], qs_sem.at[1, d], qr_sem.at[1, d], z_peer(d))
+    early = list(sent)
     attend(1, kvf, kv1)
     for d in (1, 7, 2, 6, 3, 5, 4,):
         wo_relay(1, d)
@@ -332,15 +333,18 @@
     def block(o, j, core):
         return dot_nt(o, wo[((yl + j) % NYL) * 2 + core].reshape(FEAT, HC))
 
+    def wo_collect(offsets):
+        for e in range(1, NX):
+            for d in offsets:
+                for plane in range(NYH):
+                    if (plane, d, e) in relayed:
+                        continue
+                    arrived(wo_block(plane, d, e), wxs_sem.at[plane, d, e], wxr_sem.at[plane, e, d], x_peer(e))
+
     def project(s):
         o = merge(s)
         if s == 0:
-            for e in range(1, NX):
-                for d in range(NZ):
-                    for plane in range(NYH):
-                        if (plane, d, e) in relayed:
-                            continue
-                        arrived(wo_block(plane, d, e), wxs_sem.at[plane, d, e], wxr_sem.at[plane, e, d], x_peer(e))
+            wo_collect((3, 5, 4))
         for j in (2, 1, 3, 0):
             e0s[s, j] = block(o, j, 1 - c).astype(BF16)
             send(e0s.at[s, j], e0r.at[s, j], e0s_sem.at[s, j], e0r_sem.at[s, j], sibling)
@@ -354,6 +358,9 @@
             else:
                 acc[s] = mine
 
+    for copy in early:
+        copy.wait_send()
+    wo_collect((0, 1, 7, 2, 6))
     project(0)
     project(1)
     for s in range(2):
@@ -363,7 +370,7 @@
             total = total + e1r[s, j].astype(F32)
         out_ref[s * TOK : (s + 1) * TOK] = (gates[s] * total).astype(BF16)
 
-    for copy in sent:
+    for copy in sent[len(early) :]:
         copy.wait_send()
 
 

time: 54.3 us -> 54.1 us (level)
  no operation moved by 1% of the time
where the time goes in v7:
time: 54.1 us; the launch traced here: 53.9 us
  Pallas kernels  51.9 us (96%)
  local copies, waits for them, and re-layouts  1.42 us (3%)
  between operations  0.66 us (1%)
    pallas_call x1, Pallas kernels, body(): pl.pallas_call(kernel, out_shape=jax.ShapeDtypeStruct((2 * TOK, FEAT), BF...  51.9 us
    unnamed x1, local copies, waits for them, and re-layouts  1.42 us

profile of v7, /device:TPU:1, one launch (start us, length us, event | category | flops | bytes accessed | tf_op | source)
XLA Modules:
  0.0 53.9 jit_solution(8667147416813357731)
XLA Ops:
  0.7 51.9 %block.1 = bf16[64,384]{1,0:T(8,128)(2,1)} custom-call(bf16[2,32,384]{2,1,0:T(8,128)(2,1)} %x_ref.1, bf16[2,32,256]{2,1,0:T(8,128)(2,1)} %stale_ref.1, bf16[3,3072,256]{2,1,0:T(8,128)(2,1)} %bitcast.4, bf16[48,256]{1,0:T(8,128)(2,1)} %bitcast.6, f32[3,4,384]{2,1,0:T(4,128)} %bitcast.7, s32[2]{0:T(128)} %ids_ref.1, s32[1]{0:T(128)S(6)} %copy.9.order_ref), custom_call_target="tpu_custom_call" | custom-call | tf_op jit(solution)/shard_map/block/pallas_call | solution.py:380
  52.5 1.4 %copy.10 = bf16[2,32,384]{2,1,0:T(8,128)(2,1)} copy(bf16[2,32,384]{2,1,0:T(8,128)(2,1)} %bitcast.5) | data formatting | bytes 98304
